TPU v7x, 32 devices: a whole 2x2x4 slice. The times are simulated.
32 devices in a mesh: dp: 16 (over z, y, core), mp: 2 (over x).
Axes of the slice: x: 2, y: 2, z: 4, core: 2. Of those that a mesh axis runs over, the one named last changes fastest.
Arguments:
- queries: bfloat16 [12288, 6144], P('dp', 'mp'), may hold values from -20 to 20
- keys: bfloat16 [12288, 6144], P('dp', 'mp'), may hold values from -20 to 20
- values: bfloat16 [12288, 6144], P('dp', 'mp'), may hold values from -12 to 12
- patch_counts: int32 [64], replicated, may hold values from 1 to 768, 12288 in all
- out_weight: bfloat16 [6144, 6144], P('mp', 'dp'), may hold values from -0.078125 to 0.078125
Outputs:
- projected: bfloat16 [12288, 6144], P(('dp', 'mp'))
Inputs may be any that keep to these rules, and one draw needn't show every extreme that they name: `patch_counts`: the counts sum to 12288; the largest is exactly 768.
All inputs are finite; a program needn't handle non-finite values.
Results may differ from a plain program's by a relative error of at most 0.0066.
Values may be sent and summed in bfloat16 or wider, within the bound.
A program may use at most 256 MiB of HBM per device.

v0:
```python
import jax
import jax.numpy as jnp
from jax import lax
from jax.sharding import PartitionSpec as P

HEAD_DIM = 128


def extended(value, sides, width):
    for axis, dim in sides:
        devices, length = (lax.axis_size(axis), value.shape[dim])
        up = [(i, (i + 1) % devices) for i in range(devices - 1)]
        down = [(j, i) for i, j in up]
        last = lax.slice_in_dim(value, length - width, length, axis=dim)
        initial = lax.slice_in_dim(value, 0, width, axis=dim)
        before = lax.ppermute(last, axis, up)
        after = lax.ppermute(initial, axis, down)
        value = jnp.concatenate([before, value, after], axis=dim)
    return value


def image_index(positions, starts):
    return jnp.sum((starts[None, :] <= positions[:, None]).astype(jnp.int32), axis=1) - 1


def attend_block(q_block, k_window, v_window, same_image):
    head_count = q_block.shape[1] // HEAD_DIM

    def one_head(head_index):
        q_head = lax.dynamic_slice_in_dim(q_block, head_index * HEAD_DIM, HEAD_DIM, 1)
        k_head = lax.dynamic_slice_in_dim(k_window, head_index * HEAD_DIM, HEAD_DIM, 1)
        v_head = lax.dynamic_slice_in_dim(v_window, head_index * HEAD_DIM, HEAD_DIM, 1)
        scores = jnp.dot(q_head, k_head.T, preferred_element_type=jnp.float32) * HEAD_DIM ** (-0.5)
        scores = jnp.where(same_image, scores, jnp.float32(-1e30))
        row_max = jnp.max(scores, axis=1, keepdims=True)
        lifted = jnp.exp(scores - row_max)
        row_total = jnp.sum(lifted, axis=1, keepdims=True)
        weights = (lifted / row_total).astype(jnp.bfloat16)
        return jnp.dot(weights, v_head, preferred_element_type=jnp.float32).astype(jnp.bfloat16)

    per_head = lax.map(one_head, jnp.arange(head_count))
    return jnp.transpose(per_head, (1, 0, 2)).reshape(q_block.shape[0], head_count * HEAD_DIM)


def shards(queries, keys, values, patch_counts, out_weight):
    tok_rows = queries.shape[0]
    kv_pair = jnp.stack([keys, values])
    padded = extended(kv_pair, (("dp", 1),), tok_rows)
    row_first = lax.axis_index("dp") * tok_rows
    total_rows = lax.axis_size("dp") * tok_rows
    starts = jnp.cumsum(patch_counts) - patch_counts
    q_pos = row_first + jnp.arange(tok_rows)
    k_pos = row_first - tok_rows + jnp.arange(3 * tok_rows)
    k_valid = (k_pos >= 0) & (k_pos < total_rows)
    same_image = (
        image_index(q_pos, starts)[:, None] == image_index(k_pos, starts)[None, :]
    ) & k_valid[None, :]
    attended = attend_block(queries, padded[0], padded[1], same_image)
    partial_value = jnp.dot(
        attended,
        lax.all_gather(out_weight, "dp", axis=1, tiled=True),
        preferred_element_type=jnp.float32,
    )
    summed = lax.psum_scatter(
        partial_value.astype(jnp.bfloat16), "mp", scatter_dimension=0, tiled=True
    )
    return summed


def solution(mesh):
    placed = (P("dp", "mp"), P("dp", "mp"), P("dp", "mp"), P(), P("mp", "dp"))
    return jax.shard_map(
        shards, mesh=mesh, in_specs=placed, out_specs=P(("dp", "mp"), None), check_vma=False
    )
```

profile of v0, /device:TPU:1, one launch (start us, length us, event | category | flops | bytes accessed | tf_op | source)
XLA Modules:
  0.0 812.9 jit_solution(10054850859193327377)
XLA Ops:
  7.3 8.2 %pad_maximum_fusion.1 = bf16[2,768,3072]{2,1,0:T(8,128)(2,1)} fusion(bf16[1,768,3072]{2,1,0:T(8,128)(2,1)} %bitcast.19, bf16[1,768,3072]{2,1,0:T(8,128)(2,1)} %bitcast.21), kind=kLoop, calls=%fused_computation.18 | loop fusion | flops 4718592 | bytes 18874368 | tf_op jit(solution)/shard_map/stack | solution.py:47
  15.6 4.5 collective-permute-start
  20.1 3.7 collective-permute-start.1
  24.4 372.5 %collective-permute-done = bf16[2,768,3072]{2,1,0:T(8,128)(2,1)} collective-permute-done((bf16[2,768,3072]{2,1,0:T(8,128)(2,1)}, bf16[2,768,3072]{2,1,0:T(8,128)(2,1)}, u32[]{:S(2)}, u32[]{:S(2)}) %collective-permute-start) | collective-permute-done | bytes 9437216 | tf_op jit(solution)/shard_map/ppermute | solution.py:16
  397.0 20.0 %pad_maximum_fusion = bf16[2,2304,3072]{2,1,0:T(8,128)(2,1)} fusion(bf16[2,768,3072]{2,1,0:T(8,128)(2,1)} %collective-permute-done.1, bf16[1,768,3072]{2,1,0:T(8,128)(2,1)} %bitcast.20, bf16[1,768,3072]{2,1,0:T(8,128)(2,1)} %bitcast.22, bf16[2,768,3072]{2,1,0:T(8,128)(2,1)} %collective-permute-done), kind=kLoop, calls=%fused_computation.14 | loop fusion | flops 113246208 | bytes 56623104 | tf_op jit(solution)/shard_map/concatenate | solution.py:18
  417.0 20.5 %slice_bitcast_fusion = (bf16[2304,3072]{1,0:T(8,128)(2,1)}, bf16[2304,3072]{1,0:T(8,128)(2,1)}) fusion(bf16[2,2304,3072]{2,1,0:T(8,128)(2,1)} %pad_maximum_fusion), kind=kLoop, calls=%fused_computation.15 | loop fusion | bytes 56623104 | tf_op jit(solution)/shard_map/squeeze | solution.py:58
  437.4 220.5 %while.11 = (s32[]{:T(128)}, bf16[24,768,128]{1,2,0:T(8,128)(2,1)}, s32[24]{0:T(128)S(1)}, bf16[768,3072]{1,0:T(8,128)(2,1)}, bf16[2304,3072]{1,0:T(8,128)(2,1)}...) while((s32[]{:T(128)}, bf16[24,768,128]{1,2,0:T(8,128)(2,1)}, ...), condition=%wide.region_6.7_spmd.clone, body=%wide.region_3.6_spmd.clone.sunk | while | flops 923761152 | bytes 23624636 | solution.py:41
  438.7 3.1 fusion.19
  447.9 3.1 fusion.19
  457.0 3.2 fusion.19
  466.2 3.2 fusion.19
  475.4 3.2 fusion.19
  484.6 3.2 fusion.19
  493.8 3.2 fusion.19
  503.0 3.2 fusion.19
  512.2 3.2 fusion.19
  521.4 3.2 fusion.19
  530.5 3.2 fusion.19
  548.9 3.2 fusion.19
  558.1 3.2 fusion.19
  567.3 3.2 fusion.19
  576.5 3.2 fusion.19
  585.6 3.2 fusion.19
  594.8 3.2 fusion.19
  604.0 3.2 fusion.19
  613.2 3.2 fusion.19
  622.4 3.2 fusion.19
  631.6 3.2 fusion.19
  640.8 3.2 fusion.19
  650.0 3.2 fusion.19
  657.9 36.1 %convolution_convert_fusion = bf16[768,6144]{1,0:T(8,128)(2,1)} fusion(bf16[768,3072]{0,1:T(8,128)(2,1)} %bitcast.24, bf16[3072,6144]{1,0:T(8,128)(2,1)} %all-gather.2.cloned.1.call-done), kind=kOutput, calls=%fused_computation.17 | convolution fusion | flops 28995747840 | bytes 51904512 | tf_op jit(solution)/shard_map/dot_general | solution.py:59
  694.0 112.1 %reduce-scatter.2.cloned.1.call-done = bf16[384,6144]{1,0:T(8,128)(2,1)} async-done(((bf16[768,6144]{1,0:T(8,128)(2,1)}), bf16[384,6144]{1,0:T(8,128)(2,1)}) %reduce-scatter.2.cloned.1.call-update) | async-done | bytes 4718608 | tf_op jit(solution)/shard_map/reduce_scatter | solution.py:64
  (142 shorter events, 133.6 us)
Async XLA Ops:
  6.5 651.4 %all-gather.2.cloned.1.call-start = ((), (), s32[]{:S(2)}) async-start(), calls=%async_computation.1 | async-start | bytes 40108032 | tf_op jit(solution)/shard_map/all_gather | solution.py:61
  7.3 798.8 %reduce-scatter.2.cloned.1.call-start = ((), (), s32[]{:S(2)}) async-start(), calls=%async_computation.2 | async-start | bytes 14155776 | tf_op jit(solution)/shard_map/reduce_scatter | solution.py:64
  7.3 16.5 %copy-start = (s32[64]{0:T(128)S(1)}, s32[64]{0:T(128)}, u32[]{:S(2)}) copy-start(s32[64]{0:T(128)} %param.10) | copy-start | bytes 772
  15.6 381.4 %collective-permute-start = (bf16[2,768,3072]{2,1,0:T(8,128)(2,1)}, bf16[2,768,3072]{2,1,0:T(8,128)(2,1)}, u32[]{:S(2)}, u32[]{:S(2)}) collective-permute-start(bf16[2,768,3072]{2,1,0:T(8,128)(2,1)} %pad_maximum_fusion.1), channel_id=1, source_target_pairs={{0,2},{2,4},{4,6},{6,8},{8,10},{10,12},{12,14},{14,16},{16,18},{18... | collective-permute-start | bytes 28311560 | tf_op jit(solution)/shard_map/ppermute | solution.py:16
  20.1 376.9 %collective-permute-start.1 = (bf16[2,768,3072]{2,1,0:T(8,128)(2,1)}, bf16[2,768,3072]{2,1,0:T(8,128)(2,1)}, u32[]{:S(2)}, u32[]{:S(2)}) collective-permute-start(bf16[2,768,3072]{2,1,0:T(8,128)(2,1)} %pad_maximum_fusion.1), channel_id=1, source_target_pairs={{2,0},{4,2},{6,4},{8,6},{10,8},{12,10},{14,12},{16,14},{18,16},{20... | collective-permute-start | bytes 28311560 | tf_op jit(solution)/shard_map/ppermute | solution.py:17
Sparse Core Ops, SparseCore 0:
  8.9 373.7 all-gather.1
  694.1 111.9 reduce-scatter.1
where the time goes:
time: 816 us; the launch traced here: 813 us
  waiting for transfers between devices  485 us (59%)
  matrix products  180 us (22%)
  other arithmetic  55.1 us (7%)
  local copies, waits for them, and re-layouts  55 us (7%)
  loops' own time  15.6 us (2%)
  between operations  13.5 us (2%)
  starting transfers between devices  8.23 us (1%)
    ppermute x1, waiting for transfers between devices, extended(): before = lax.ppermute(last, axis, up)  373 us
    reduce_scatter x1, waiting for transfers between devices, shards(): lax.psum_scatter(partial_value.astype(jnp.bfloat16), 'mp', scatter_dimens...  112 us
    dot_general x24, matrix products, one_head(): jnp.dot(q_head, k_head.T, preferred_element_type=jnp.float32)  75.7 us
    dot_general x24, matrix products, one_head(): jnp.dot(weights, v_head, preferred_element_type=jnp.float32)  68.3 us
    dot_general x1, matrix products, shards(): jnp.dot(attended, lax.all_gather(out_weight, 'dp', axis=1, tiled=True), p...  36.1 us
    reduce_sum x24, other arithmetic, one_head(): row_total = jnp.sum(lifted, axis=1, keepdims=True)  26.4 us
    squeeze x1, local copies, waits for them, and re-layouts, shards(): attended = attend_block(queries, padded[0], padded[1], same_image)  20.5 us
    dynamic_update_slice x48, local copies, waits for them, and re-layouts, attend_block(): per_head = lax.map(one_head, jnp.arange(head_count))  20.2 us
  transfers between devices with their start and end apart: 4, of which 2 were waited for; matrix products, arithmetic and copies ran while one was open for 31% of the time, Pallas kernels for 0%

commit v1 on v0

v1 whole, which is shorter than its diff:
```python
import functools

import jax
import jax.numpy as jnp
from jax import lax
from jax.experimental import pallas as pl
from jax.experimental.pallas import tpu as pltpu
from jax.sharding import PartitionSpec as P

HEAD_DIM = 128
Q_ROWS = 256
K_ROWS = 256
CHUNKS = 3
LOG2E = 1.4426950408889634


def attend_kernel(span_ref, q_ref, kb_ref, k_ref, ka_ref, vb_ref, v_ref, va_ref, qseg_ref, kseg_ref, out_ref,
                  acc_ref, max_ref, *, heads, rows):
    factor = HEAD_DIM ** (-0.5) * LOG2E
    per_part = rows // K_ROWS
    ones = jnp.ones((K_ROWS, HEAD_DIM), jnp.bfloat16)

    def q_step(qi, _):
        q_at = pl.ds(pl.multiple_of(qi * Q_ROWS, Q_ROWS), Q_ROWS)
        acc_ref[...] = jnp.zeros_like(acc_ref)
        max_ref[...] = jnp.full_like(max_ref, -1e30)
        qseg = qseg_ref[q_at, :]
        qseg = jnp.concatenate([qseg] * (K_ROWS // 128), axis=1)
        low, high = span_ref[0, qi], span_ref[1, qi]

        for part, (kk, vv) in enumerate(((kb_ref, vb_ref), (k_ref, v_ref), (ka_ref, va_ref))):
            def k_step(ki, _, part=part, kk=kk, vv=vv):
                k_at = pl.ds(pl.multiple_of(ki * K_ROWS, K_ROWS), K_ROWS)
                same = qseg == kseg_ref[part * per_part + ki]
                for h in range(heads):
                    cols = pl.ds(h * HEAD_DIM, HEAD_DIM)
                    s = lax.dot_general(q_ref[q_at, cols], kk[k_at, cols], (((1,), (1,)), ((), ())),
                                        preferred_element_type=jnp.float32) * factor
                    s = jnp.where(same, s, -1e30)
                    old = max_ref[h]
                    new = jnp.maximum(old, jnp.max(s, axis=1, keepdims=True))
                    max_ref[h] = new
                    wide = jnp.concatenate([new] * (K_ROWS // 128), axis=1)
                    p = jnp.exp2(s - wide).astype(jnp.bfloat16)
                    fade = jnp.exp2(old - new)
                    v_ext = jnp.concatenate([vv[k_at, cols], ones], axis=1)
                    acc_ref[h] = acc_ref[h] * jnp.concatenate([fade, fade], axis=1) + jnp.dot(
                        p, v_ext, preferred_element_type=jnp.float32)
                return 0

            first = jnp.clip(low - part * per_part, 0, per_part)
            last = jnp.clip(high - part * per_part, 0, per_part)
            lax.fori_loop(first, last, k_step, 0)
        for h in range(heads):
            acc = acc_ref[h]
            out_ref[q_at, h * HEAD_DIM:(h + 1) * HEAD_DIM] = (
                acc[:, :HEAD_DIM] / acc[:, HEAD_DIM:]).astype(jnp.bfloat16)
        return 0

    lax.fori_loop(0, rows // Q_ROWS, q_step, 0)


def attend(span, queries, keys, values, before, after, q_seg, k_seg, chunk, width):
    rows = queries.shape[0]
    heads = next(n for n in (4, 3, 2, 1) if (width // HEAD_DIM) % n == 0)
    block = heads * HEAD_DIM
    steps = width // block
    whole = pl.BlockSpec((rows, block), lambda i, s: (0, chunk * steps + i))
    k_part = pl.BlockSpec((rows, block), lambda i, s: (0, i))
    v_part = pl.BlockSpec((rows, block), lambda i, s: (0, steps + i))
    return pl.pallas_call(
        functools.partial(attend_kernel, heads=heads, rows=rows),
        grid_spec=pltpu.PrefetchScalarGridSpec(
            num_scalar_prefetch=1,
            grid=(steps,),
            in_specs=[whole, k_part, whole, k_part, v_part, whole, v_part,
                      pl.BlockSpec((rows, 128), lambda i, s: (0, 0)),
                      pl.BlockSpec((3 * rows // K_ROWS, 1, K_ROWS), lambda i, s: (0, 0, 0))],
            out_specs=pl.BlockSpec((rows, block), lambda i, s: (0, i)),
            scratch_shapes=[pltpu.VMEM((heads, Q_ROWS, 2 * HEAD_DIM), jnp.float32),
                            pltpu.VMEM((heads, Q_ROWS, HEAD_DIM), jnp.float32)],
        ),
        out_shape=jax.ShapeDtypeStruct((rows, width), jnp.bfloat16),
        compiler_params=pltpu.CompilerParams(vmem_limit_bytes=40 * 2 ** 20),
        cost_estimate=pl.CostEstimate(flops=4 * rows * rows * width, bytes_accessed=16 * rows * width,
                                      transcendentals=rows * rows * width // HEAD_DIM),
    )(span, queries, before, keys, after, before, values, after, q_seg, k_seg)


def shards(queries, keys, values, patch_counts, out_weight):
    rows, columns = queries.shape
    devices, groups = lax.axis_size("dp"), lax.axis_size("mp")
    width = columns // CHUNKS
    up = [(i, i + 1) for i in range(devices - 1)]
    down = [(j, i) for i, j in up]

    halos = []
    for c in range(CHUNKS):
        at = slice(c * width, (c + 1) * width)
        pair = jnp.concatenate([keys[:, at], values[:, at]], axis=1)
        if halos:
            pair, _ = lax.optimization_barrier((pair, halos[-1][0][:8, :128]))
        halos.append((lax.ppermute(pair, "dp", up), lax.ppermute(pair, "dp", down)))

    row_first = lax.axis_index("dp") * rows
    total_rows = devices * rows
    ends = jnp.cumsum(patch_counts)
    starts = ends - patch_counts
    k_pos = row_first - rows + jnp.arange(3 * rows, dtype=jnp.int32)
    seg = jnp.sum((starts[None, :] <= k_pos[:, None]).astype(jnp.int32), axis=1) - 1
    seg = jnp.where((k_pos >= 0) & (k_pos < total_rows), seg, -1)
    q_seg = jnp.broadcast_to(seg[rows:2 * rows, None], (rows, 128))
    k_seg = seg.reshape(3 * rows // K_ROWS, 1, K_ROWS)
    q_first = row_first + jnp.arange(rows // Q_ROWS, dtype=jnp.int32) * Q_ROWS
    low = jnp.max(jnp.where(starts[None, :] <= q_first[:, None], starts[None, :], 0), axis=1)
    q_last = q_first + Q_ROWS - 1
    high = jnp.min(jnp.where(ends[None, :] > q_last[:, None], ends[None, :], total_rows), axis=1)
    low = jnp.clip((low - row_first + rows) // K_ROWS, 0, 3 * rows // K_ROWS)
    high = jnp.clip((high - row_first + rows + K_ROWS - 1) // K_ROWS, 0, 3 * rows // K_ROWS)
    span = jnp.stack([low, high]).astype(jnp.int32)

    attended = jnp.concatenate(
        [attend(span, queries, keys, values, *halos[c], q_seg, k_seg, c, width) for c in range(CHUNKS)], axis=1)

    part = out_weight.shape[1] // CHUNKS
    block = rows // groups
    me = lax.axis_index("mp")
    done = []
    for c in range(CHUNKS):
        piece = out_weight[:, c * part:(c + 1) * part]
        if c == 1:
            piece, _ = lax.optimization_barrier((piece, halos[-1][0][:8, :128]))
        gathered = lax.all_gather(piece, "dp", axis=1, tiled=True)
        partial_value = jnp.dot(attended, gathered, preferred_element_type=jnp.float32).astype(jnp.bfloat16)
        total = lax.dynamic_slice_in_dim(partial_value, me * block, block, 0).astype(jnp.float32)
        for k in range(1, groups):
            theirs = lax.dynamic_slice_in_dim(partial_value, ((me + k) % groups) * block, block, 0)
            got = lax.ppermute(theirs, "mp", [(i, (i + k) % groups) for i in range(groups)])
            total = total + got.astype(jnp.float32)
        done.append(total.astype(jnp.bfloat16).reshape(block, devices, 1, part))
    return jnp.concatenate(done, axis=2).reshape(block, devices * CHUNKS * part)


def solution(mesh):
    placed = (P("dp", "mp"), P("dp", "mp"), P("dp", "mp"), P(), P("mp", "dp"))
    return jax.shard_map(
        shards, mesh=mesh, in_specs=placed, out_specs=P(("dp", "mp"), None), check_vma=False
    )
```

time: 816 us -> 531 us (0.65)
  matrix products: 180 us -> 40.2 us
  waiting for transfers between devices: 485 us -> 350 us
  Pallas kernels: 0 us -> 51.1 us
  other arithmetic: 55.1 us -> 20.2 us
  local copies, waits for them, and re-layouts: 55 us -> 33.1 us
  loops' own time: 15.6 us -> 0 us
  starting transfers between devices: 8.23 us -> 21.6 us
    ppermute x2 -> x9, waiting for transfers between devices: 373 us -> 222 us  [the longest x6 196 us: shards(): halos.append((lax.ppermute(pair, 'dp', up), lax.ppermute(pair, 'dp', down)))]
    dot_general x49 -> x3, matrix products: 180 us -> 40.2 us  [shards(): jnp.dot(attended, gathered, preferred_element_type=jnp.float32)]
    all_gather x1 -> x3, waiting for transfers between devices: 0.01 us -> 127 us  [shards(): gathered = lax.all_gather(piece, 'dp', axis=1, tiled=True)]
    reduce_scatter x1 -> x0, waiting for transfers between devices: 112 us -> none  [shards(): lax.psum_scatter(partial_value.astype(jnp.bfloat16), 'mp', scatter_dimens...]
    pallas_call x0 -> x3, Pallas kernels: none -> 51.1 us  [attend(): pl.pallas_call(functools.partial(attend_kernel, heads=heads, rows=rows),...]
    reduce_sum x26 -> x1, other arithmetic: 26.6 us -> 0.15 us  [shards(): jnp.sum((starts[None, :] <= k_pos[:, None]).astype(jnp.int32), axis=1) - 1]
    squeeze x1 -> x0, local copies, waits for them, and re-layouts: 20.5 us -> none  [shards(): attended = attend_block(queries, padded[0], padded[1], same_image)]
    dynamic_update_slice x48 -> x0, local copies, waits for them, and re-layouts: 20.2 us -> none  [attend_block(): per_head = lax.map(one_head, jnp.arange(head_count))]
  transfers between devices with their start and end apart: 4 -> 12, of which waited for: 2 -> 6; matrix products, arithmetic and copies ran while one was open for 31% -> 12% of each run, Pallas kernels for 0% -> 10%
where the time goes in v1:
time: 531 us; the launch traced here: 530 us
  waiting for transfers between devices  350 us (66%)
  Pallas kernels  51.1 us (10%)
  matrix products  40.2 us (8%)
  local copies, waits for them, and re-layouts  33.1 us (6%)
  starting transfers between devices  21.6 us (4%)
  other arithmetic  20.2 us (4%)
  between operations  13.4 us (3%)
    ppermute x6, waiting for transfers between devices, shards(): halos.append((lax.ppermute(pair, 'dp', up), lax.ppermute(pair, 'dp', down)))  196 us
    all_gather x3, waiting for transfers between devices, shards(): gathered = lax.all_gather(piece, 'dp', axis=1, tiled=True)  127 us
    pallas_call x3, Pallas kernels, attend(): pl.pallas_call(functools.partial(attend_kernel, heads=heads, rows=rows),...  51.1 us
    dot_general x3, matrix products, shards(): jnp.dot(attended, gathered, preferred_element_type=jnp.float32)  40.2 us
    ppermute x3, waiting for transfers between devices, shards(): lax.ppermute(theirs, 'mp', [(i, (i + k) % groups) for i in range(groups)])  25.9 us
    ppermute x6, starting transfers between devices, shards(): halos.append((lax.ppermute(pair, 'dp', up), lax.ppermute(pair, 'dp', down)))  17.7 us
  transfers between devices with their start and end apart: 12, of which 6 were waited for; matrix products, arithmetic and copies ran while one was open for 12% of the time, Pallas kernels for 10%

profile of v1, /device:TPU:1, one launch (start us, length us, event | category | flops | bytes accessed | tf_op | source)
XLA Modules:
  0.0 530.0 jit_solution(10587038044412283213)
XLA Ops:
  6.5 3.0 fusion.4
  11.1 4.3 fusion.2
  15.4 1.9 pad_maximum_fusion.2
  17.3 4.5 collective-permute-start
  21.8 1.9 collective-permute-start.1
  23.7 2.1 pad_maximum_fusion.3
  25.8 3.6 collective-permute-start.2
  29.4 2.3 collective-permute-start.3
  31.7 2.0 pad_maximum_fusion.4
  33.7 3.3 collective-permute-start.4
  37.0 132.6 %collective-permute-done.kb_ref.vb_ref = bf16[768,2048]{1,0:T(8,128)(2,1)S(1)} collective-permute-done((bf16[768,2048]{1,0:T(8,128)(2,1)}, bf16[768,2048]{1,0:T(8,128)(2,1)S(1)}, u32[]{:S(2)}, u32[]{:S(2)}) %collective-permute-start) | collective-permute-done | bytes 3145760 | tf_op jit(solution)/shard_map/ppermute | solution.py:103
  169.5 2.1 collective-permute-start.5
  172.8 2.5 copy-done
  175.4 16.8 %shard_map.55 = bf16[768,1024]{1,0:T(8,128)(2,1)S(1)} custom-call(s32[2,3]{1,0:T(2,128)S(1)} %pad_add_fusion.span_ref, bf16[768,3072]{1,0:T(8,128)(2,1)S(1)} %copy-done, bf16[768,2048]{1,0:T(8,128)(2,1)S(1)} %collective-permute-done.kb_ref.vb_ref, bf16[768,3072]{1,0:T(8,128)(2,1)} %k_ref.5, bf16[768,2048]{1,0:T(8,128)(2,1)} %collective-permute-done.1.ka_ref.va_ref, ...), custom_call_target="tpu_custom_call" | custom-call | flops 2415919104 | bytes 12582912 | tf_op jit(solution)/shard_map/pallas_call | solution.py:71
  193.3 38.3 %collective-permute-done.2.kb_ref.vb_ref = bf16[768,2048]{1,0:T(8,128)(2,1)} collective-permute-done((bf16[768,2048]{1,0:T(8,128)(2,1)}, bf16[768,2048]{1,0:T(8,128)(2,1)}, u32[]{:S(2)}, u32[]{:S(2)}) %collective-permute-start.2) | collective-permute-done | bytes 3145760 | tf_op jit(solution)/shard_map/ppermute | solution.py:103
  231.6 17.1 %shard_map.56 = bf16[768,1024]{1,0:T(8,128)(2,1)S(1)} custom-call(s32[2,3]{1,0:T(2,128)S(1)} %pad_add_fusion.span_ref, bf16[768,3072]{1,0:T(8,128)(2,1)S(1)} %copy-done, bf16[768,2048]{1,0:T(8,128)(2,1)} %collective-permute-done.2.kb_ref.vb_ref, bf16[768,3072]{1,0:T(8,128)(2,1)} %k_ref.5, bf16[768,2048]{1,0:T(8,128)(2,1)} %collective-permute-done.3.ka_ref.va_ref, ...), custom_call_target="tpu_custom_call" | custom-call | flops 2415919104 | bytes 12582912 | tf_op jit(solution)/shard_map/pallas_call | solution.py:71
  248.8 25.0 %collective-permute-done.4.kb_ref.vb_ref = bf16[768,2048]{1,0:T(8,128)(2,1)} collective-permute-done((bf16[768,2048]{1,0:T(8,128)(2,1)}, bf16[768,2048]{1,0:T(8,128)(2,1)}, u32[]{:S(2)}, u32[]{:S(2)}) %collective-permute-start.4) | collective-permute-done | bytes 3145760 | tf_op jit(solution)/shard_map/ppermute | solution.py:103
  273.7 17.2 %shard_map.57 = bf16[768,1024]{1,0:T(8,128)(2,1)S(1)} custom-call(s32[2,3]{1,0:T(2,128)S(1)} %pad_add_fusion.span_ref, bf16[768,3072]{1,0:T(8,128)(2,1)S(1)} %copy-done, bf16[768,2048]{1,0:T(8,128)(2,1)} %collective-permute-done.4.kb_ref.vb_ref, bf16[768,3072]{1,0:T(8,128)(2,1)} %k_ref.5, bf16[768,2048]{1,0:T(8,128)(2,1)} %collective-permute-done.5.ka_ref.va_ref, ...), custom_call_target="tpu_custom_call" | custom-call | flops 2415919104 | bytes 12582912 | tf_op jit(solution)/shard_map/pallas_call | solution.py:71
  292.1 13.6 %convolution_convert_fusion.2 = bf16[768,2048]{1,0:T(8,128)(2,1)S(1)} fusion(bf16[3072,2048]{1,0:T(8,128)(2,1)} %all-gather.4.cloned.1.call-done, bf16[768,1024]{1,0:T(8,128)(2,1)} %copy-done.3, bf16[768,1024]{1,0:T(8,128)(2,1)S(1)} %shard_map.56, bf16[768,1024]{1,0:T(8,128)(2,1)S(1)} %copy-done.2), kind=kOutput, calls=%fused_computation.4 | convolution fusion | flops 9679405056 | bytes 20447232 | tf_op jit(solution)/shard_map/dot_general | solution.py:134
  305.6 1.7 copy-done.4
  310.0 40.3 %all-gather.6.cloned.1.call-done = bf16[3072,2048]{1,0:T(8,128)(2,1)} async-done(((bf16[3072,128]{1,0:T(8,128)(2,1)}), bf16[3072,2048]{1,0:T(8,128)(2,1)}) %all-gather.6.cloned.1.call-update) | async-done | bytes 12582928 | tf_op jit(solution)/shard_map/all_gather | solution.py:133
  350.3 13.3 %convolution_convert_fusion.1 = bf16[768,2048]{1,0:T(8,128)(2,1)S(1)} fusion(bf16[3072,2048]{1,0:T(8,128)(2,1)} %all-gather.6.cloned.1.call-done, bf16[768,1024]{1,0:T(8,128)(2,1)} %copy-done.3, bf16[768,1024]{1,0:T(8,128)(2,1)S(1)} %shard_map.56, bf16[768,1024]{1,0:T(8,128)(2,1)S(1)} %copy-done.2), kind=kOutput, calls=%fused_computation.3 | convolution fusion | flops 9679405056 | bytes 20447232 | tf_op jit(solution)/shard_map/dot_general | solution.py:134
  367.7 86.9 %all-gather.8.cloned.1.call-done = bf16[3072,2048]{1,0:T(8,128)(2,1)} async-done(((bf16[3072,128]{1,0:T(8,128)(2,1)}), bf16[3072,2048]{1,0:T(8,128)(2,1)}) %all-gather.8.cloned.1.call-update) | async-done | bytes 12582928 | tf_op jit(solution)/shard_map/all_gather | solution.py:133
  454.6 13.3 %convolution_convert_fusion = bf16[768,2048]{1,0:T(8,128)(2,1)S(1)} fusion(bf16[3072,2048]{1,0:T(8,128)(2,1)} %all-gather.8.cloned.1.call-done, bf16[768,1024]{1,0:T(8,128)(2,1)} %copy-done.3, bf16[768,1024]{1,0:T(8,128)(2,1)S(1)} %shard_map.56, bf16[768,1024]{1,0:T(8,128)(2,1)S(1)} %copy-done.2), kind=kOutput, calls=%fused_computation.2 | convolution fusion | flops 9679405056 | bytes 20447232 | tf_op jit(solution)/shard_map/dot_general | solution.py:134
  472.1 2.5 add_convert_fusion.2
  475.5 3.7 add_convert_fusion.1
  479.2 1.9 copy.19
  481.1 25.9 %collective-permute-done.8 = bf16[384,2048]{1,0:T(8,128)(2,1)} collective-permute-done((bf16[384,2048]{1,0:T(8,128)(2,1)}, bf16[384,2048]{1,0:T(8,128)(2,1)}, u32[]{:S(2)}, u32[]{:S(2)}) %collective-permute-start.8) | collective-permute-done | bytes 1572896 | tf_op jit(solution)/shard_map/ppermute | solution.py:138
  507.0 3.7 add_convert_fusion
  510.7 2.6 copy.20
  513.3 3.6 pad_maximum_fusion.1
  516.8 6.6 %copy.17 = bf16[384,6144]{1,0:T(8,128)(2,1)} copy(bf16[384,6144]{0,1:T(8,128)(2,1)} %bitcast.28) | data formatting | bytes 9437184 | tf_op jit(solution)/shard_map/reshape | solution.py:141
  (50 shorter events, 16.6 us)
Async XLA Ops:
  6.5 285.5 %all-gather.4.cloned.1.call-start = ((), (), s32[]{:S(2)}) async-start(), calls=%async_computation | async-start | bytes 13369344 | tf_op jit(solution)/shard_map/all_gather | solution.py:133
  9.6 340.7 %all-gather.6.cloned.1.call-start = ((), (), s32[]{:S(2)}) async-start(), calls=%async_computation.1 | async-start | bytes 13369344 | tf_op jit(solution)/shard_map/all_gather | solution.py:133
  10.4 444.3 %all-gather.8.cloned.1.call-start = ((), (), s32[]{:S(2)}) async-start(), calls=%async_computation.2 | async-start | bytes 13369344 | tf_op jit(solution)/shard_map/all_gather | solution.py:133
  17.3 152.3 %collective-permute-start = (bf16[768,2048]{1,0:T(8,128)(2,1)}, bf16[768,2048]{1,0:T(8,128)(2,1)S(1)}, u32[]{:S(2)}, u32[]{:S(2)}) collective-permute-start(bf16[768,2048]{1,0:T(8,128)(2,1)} %pad_maximum_fusion.2), channel_id=1, source_target_pairs={{0,2},{2,4},{4,6},{6,8},{8,10},{10,12},{12,14},{14,16},{16,18},{18... | collective-permute-start | bytes 9437192 | tf_op jit(solution)/shard_map/ppermute | solution.py:103
  21.8 150.8 %collective-permute-start.1 = (bf16[768,2048]{1,0:T(8,128)(2,1)}, bf16[768,2048]{1,0:T(8,128)(2,1)}, u32[]{:S(2)}, u32[]{:S(2)}) collective-permute-start(bf16[768,2048]{1,0:T(8,128)(2,1)} %pad_maximum_fusion.2), channel_id=1, source_target_pairs={{2,0},{4,2},{6,4},{8,6},{10,8},{12,10},{14,12},{16,14},{18,16},{20... | collective-permute-start | bytes 9437192 | tf_op jit(solution)/shard_map/ppermute | solution.py:103
  25.8 205.8 %collective-permute-start.2 = (bf16[768,2048]{1,0:T(8,128)(2,1)}, bf16[768,2048]{1,0:T(8,128)(2,1)}, u32[]{:S(2)}, u32[]{:S(2)}) collective-permute-start(bf16[768,2048]{1,0:T(8,128)(2,1)} %pad_maximum_fusion.3), channel_id=1, source_target_pairs={{0,2},{2,4},{4,6},{6,8},{8,10},{10,12},{12,14},{14,16},{16,18},{18... | collective-permute-start | bytes 9437192 | tf_op jit(solution)/shard_map/ppermute | solution.py:103
  29.4 202.1 %collective-permute-start.3 = (bf16[768,2048]{1,0:T(8,128)(2,1)}, bf16[768,2048]{1,0:T(8,128)(2,1)}, u32[]{:S(2)}, u32[]{:S(2)}) collective-permute-start(bf16[768,2048]{1,0:T(8,128)(2,1)} %pad_maximum_fusion.3), channel_id=1, source_target_pairs={{2,0},{4,2},{6,4},{8,6},{10,8},{12,10},{14,12},{16,14},{18,16},{20... | collective-permute-start | bytes 9437192 | tf_op jit(solution)/shard_map/ppermute | solution.py:103
  31.7 139.9 %copy-start.7 = (s32[64]{0:T(128)S(1)}, s32[64]{0:T(128)}, u32[]{:S(2)}) copy-start(s32[64]{0:T(128)} %param.8) | copy-start | bytes 772
  33.7 240.0 %collective-permute-start.4 = (bf16[768,2048]{1,0:T(8,128)(2,1)}, bf16[768,2048]{1,0:T(8,128)(2,1)}, u32[]{:S(2)}, u32[]{:S(2)}) collective-permute-start(bf16[768,2048]{1,0:T(8,128)(2,1)} %pad_maximum_fusion.4), channel_id=1, source_target_pairs={{0,2},{2,4},{4,6},{6,8},{8,10},{10,12},{12,14},{14,16},{16,18},{18... | collective-permute-start | bytes 9437192 | tf_op jit(solution)/shard_map/ppermute | solution.py:103
  169.5 104.2 %collective-permute-start.5 = (bf16[768,2048]{1,0:T(8,128)(2,1)}, bf16[768,2048]{1,0:T(8,128)(2,1)}, u32[]{:S(2)}, u32[]{:S(2)}) collective-permute-start(bf16[768,2048]{1,0:T(8,128)(2,1)} %pad_maximum_fusion.4), channel_id=1, source_target_pairs={{2,0},{4,2},{6,4},{8,6},{10,8},{12,10},{14,12},{16,14},{18,16},{20... | collective-permute-start | bytes 9437192 | tf_op jit(solution)/shard_map/ppermute | solution.py:103
  172.8 2.5 copy-start
  192.1 1.2 copy-start.1
  248.7 43.3 %copy-start.2 = (bf16[768,1024]{1,0:T(8,128)(2,1)S(1)}, bf16[768,1024]{1,0:T(8,128)(2,1)}, u32[]{:S(2)}) copy-start(bf16[768,1024]{1,0:T(8,128)(2,1)} %copy-done.1) | copy-start | bytes 4718596
  290.9 1.1 copy-start.3
  305.6 1.7 copy-start.4
  308.6 163.5 %collective-permute-start.6 = (bf16[384,2048]{1,0:T(8,128)(2,1)}, bf16[384,2048]{1,0:T(8,128)(2,1)}, u32[]{:S(2)}, u32[]{:S(2)}) collective-permute-start(bf16[384,2048]{1,0:T(8,128)(2,1)} %constant_dynamic-slice_fusion.2), channel_id=1, source_target_pairs={{0,1},{1,0},{2,3},{3,2},{4,5},{5,4},{6,7},{7,6},{8,9},{9,8},{10,11... | collective-permute-start | bytes 4718600 | tf_op jit(solution)/shard_map/ppermute | solution.py:138
  363.6 1.6 copy-start.5
  366.5 108.9 %collective-permute-start.7 = (bf16[384,2048]{1,0:T(8,128)(2,1)}, bf16[384,2048]{1,0:T(8,128)(2,1)}, u32[]{:S(2)}, u32[]{:S(2)}) collective-permute-start(bf16[384,2048]{1,0:T(8,128)(2,1)} %constant_dynamic-slice_fusion.1), channel_id=1, source_target_pairs={{0,1},{1,0},{2,3},{3,2},{4,5},{5,4},{6,7},{7,6},{8,9},{9,8},{10,11... | collective-permute-start | bytes 4718600 | tf_op jit(solution)/shard_map/ppermute | solution.py:138
  468.0 1.7 copy-start.6
  470.9 36.1 %collective-permute-start.8 = (bf16[384,2048]{1,0:T(8,128)(2,1)}, bf16[384,2048]{1,0:T(8,128)(2,1)}, u32[]{:S(2)}, u32[]{:S(2)}) collective-permute-start(bf16[384,2048]{1,0:T(8,128)(2,1)} %constant_dynamic-slice_fusion), channel_id=1, source_target_pairs={{0,1},{1,0},{2,3},{3,2},{4,5},{5,4},{6,7},{7,6},{8,9},{9,8},{10,11... | collective-permute-start | bytes 4718600 | tf_op jit(solution)/shard_map/ppermute | solution.py:138
Sparse Core Ops, SparseCore 0:
  9.7 229.4 all-gather.3
  241.4 108.8 all-gather.5
  352.5 102.1 all-gather.7

commit v2 on v1

--- a/solution.py
+++ b/solution.py
@@ -119,26 +119,86 @@
     high = jnp.clip((high - row_first + rows + K_ROWS - 1) // K_ROWS, 0, 3 * rows // K_ROWS)
     span = jnp.stack([low, high]).astype(jnp.int32)
 
-    attended = jnp.concatenate(
-        [attend(span, queries, keys, values, *halos[c], q_seg, k_seg, c, width) for c in range(CHUNKS)], axis=1)
-
-    part = out_weight.shape[1] // CHUNKS
+    chips = devices // 2
+    ring = list(range(0, chips, 2)) + list(range(chips - 1 - chips % 2, 0, -2))
+    onward = [(ring[i], ring[(i + 1) % chips]) for i in range(chips)]
+    turn = [(2 * a, 2 * b) for a, b in onward] + [(2 * b + 1, 2 * a + 1) for a, b in onward]
+    swap = [(i, i ^ 1) for i in range(devices)]
+    part = out_weight.shape[1]
     block = rows // groups
     me = lax.axis_index("mp")
-    done = []
+
+    own, other = [], []
     for c in range(CHUNKS):
-        piece = out_weight[:, c * part:(c + 1) * part]
-        if c == 1:
-            piece, _ = lax.optimization_barrier((piece, halos[-1][0][:8, :128]))
-        gathered = lax.all_gather(piece, "dp", axis=1, tiled=True)
-        partial_value = jnp.dot(attended, gathered, preferred_element_type=jnp.float32).astype(jnp.bfloat16)
-        total = lax.dynamic_slice_in_dim(partial_value, me * block, block, 0).astype(jnp.float32)
+        own.append(attend(span, queries, keys, values, *halos[c], q_seg, k_seg, c, width))
+        other.append(lax.ppermute(own[-1], "dp", swap))
+    both = jnp.concatenate([jnp.concatenate(own, axis=1), jnp.concatenate(other, axis=1)], axis=0)
+
+    weight = out_weight
+    mine, theirs, batch = [], [], []
+    for step in range(chips):
+        if step:
+            weight = lax.ppermute(weight, "dp", turn)
+        partial_value = jnp.dot(both, weight, preferred_element_type=jnp.float32)
+        partial_value = partial_value.astype(jnp.bfloat16).reshape(2, groups, block, part)
+        total = lax.dynamic_index_in_dim(partial_value, me, 1, False).astype(jnp.float32)
         for k in range(1, groups):
-            theirs = lax.dynamic_slice_in_dim(partial_value, ((me + k) % groups) * block, block, 0)
-            got = lax.ppermute(theirs, "mp", [(i, (i + k) % groups) for i in range(groups)])
+            away = lax.dynamic_index_in_dim(partial_value, (me + k) % groups, 1, False)
+            got = lax.ppermute(away, "mp", [(i, (i + k) % groups) for i in range(groups)])
             total = total + got.astype(jnp.float32)
-        done.append(total.astype(jnp.bfloat16).reshape(block, devices, 1, part))
-    return jnp.concatenate(done, axis=2).reshape(block, devices * CHUNKS * part)
+        total = total.astype(jnp.bfloat16)
+        mine.append(total[0])
+        batch.append(total[1])
+        if step % (chips // 2) == chips // 2 - 1:
+            theirs.append(lax.ppermute(jnp.stack(batch), "dp", swap))
+            batch = []
+    mine, theirs = jnp.stack(mine), jnp.concatenate(theirs, axis=0)
+
+    place = jnp.array([ring.index(c) for c in range(chips)], jnp.int32)
+    index = lax.axis_index("dp")
+    core, at = index % 2, place[index // 2]
+    owner = jnp.arange(devices, dtype=jnp.int32)
+    ahead = (at - place[owner // 2]) % chips
+    behind = (place[owner // 2] - at) % chips
+    step_of = jnp.where(owner % 2 == 0, ahead, behind)
+    return assemble(mine, theirs, step_of, core)
+
+
+def assemble_kernel(mine_at, theirs_at, core_ref, mine_ref, theirs_ref, out_ref):
+    is_mine = pl.program_id(0) % 2 == core_ref[0]
+
+    @pl.when(is_mine)
+    def _():
+        out_ref[...] = mine_ref[0]
+
+    @pl.when(jnp.logical_not(is_mine))
+    def _():
+        out_ref[...] = theirs_ref[0]
+
+
+def assemble(mine, theirs, step_of, core):
+    chips, block, part = mine.shape
+    devices = 2 * chips
+    if part % 128:
+        owner = jnp.arange(devices, dtype=jnp.int32)
+        pieces = jnp.concatenate([mine, theirs], axis=0)
+        pieces = pieces[step_of + jnp.where(owner % 2 == core, 0, chips)]
+        return jnp.transpose(pieces, (1, 0, 2)).reshape(block, devices * part)
+    pairs = step_of.reshape(chips, 2)
+    mine_at = jnp.repeat(jnp.where(core == 0, pairs[:, 0], pairs[:, 1]), 2)
+    theirs_at = jnp.repeat(jnp.where(core == 0, pairs[:, 1], pairs[:, 0]), 2)
+    return pl.pallas_call(
+        assemble_kernel,
+        grid_spec=pltpu.PrefetchScalarGridSpec(
+            num_scalar_prefetch=3,
+            grid=(devices,),
+            in_specs=[pl.BlockSpec((1, block, part), lambda d, m, t, c: (m[d], 0, 0)),
+                      pl.BlockSpec((1, block, part), lambda d, m, t, c: (t[d], 0, 0))],
+            out_specs=pl.BlockSpec((block, part), lambda d, m, t, c: (0, d)),
+        ),
+        out_shape=jax.ShapeDtypeStruct((block, devices * part), jnp.bfloat16),
+        cost_estimate=pl.CostEstimate(flops=0, bytes_accessed=4 * block * devices * part, transcendentals=0),
+    )(mine_at, theirs_at, core[None].astype(jnp.int32), mine, theirs)
 
 
 def solution(mesh):

time: 531 us -> 496 us (0.934); the launches traced: 530 us -> 489 us
  waiting for transfers between devices: 350 us -> 268 us
  starting transfers between devices: 21.6 us -> 58.7 us
  other arithmetic: 20.2 us -> 46.9 us
  local copies, waits for them, and re-layouts: 33.1 us -> 10.9 us
  between operations: 13.4 us -> 0.79 us
  Pallas kernels: 51.1 us -> 59.8 us
    ppermute x3 -> x20, waiting for transfers between devices: 25.9 us -> 209 us  [the longest x7 179 us: shards(): weight = lax.ppermute(weight, 'dp', turn)]
    ppermute x6, waiting for transfers between devices: 196 us -> 59.2 us  [shards(): halos.append((lax.ppermute(pair, 'dp', up), lax.ppermute(pair, 'dp', down)))]
    all_gather x3 -> x0, waiting for transfers between devices: 127 us -> none  [shards(): gathered = lax.all_gather(piece, 'dp', axis=1, tiled=True)]
    ppermute x3 -> x20, starting transfers between devices: 3.81 us -> 40.4 us  [the longest x7 22.7 us: shards(): weight = lax.ppermute(weight, 'dp', turn)]
    concatenate x1 -> x2, other arithmetic: 3.56 us -> 36.4 us  [the longest x1 33 us: shards(): jnp.concatenate([jnp.concatenate(own, axis=1), jnp.concatenate(other, axi...]
    pallas_call x0 -> x1, Pallas kernels: none -> 11.7 us  [assemble(): pl.pallas_call(assemble_kernel, grid_spec=pltpu.PrefetchScalarGridSpec(nu...]
    reshape x4 -> x2, local copies, waits for them, and re-layouts: 11.9 us -> 1.19 us  [the longest x1 0.63 us: assemble(): mine_at = jnp.repeat(jnp.where(core == 0, pairs[:, 0], pairs[:, 1]), 2)]
    convert_element_type x3 -> x8, other arithmetic: 9.93 us -> 1.2 us  [shards(): total = total.astype(jnp.bfloat16)]
  transfers between devices with their start and end apart: 12 -> 26, of which waited for: 6 -> 12; matrix products, arithmetic and copies ran while one was open for 12% -> 18% of each run, Pallas kernels for 10% -> 10%
where the time goes in v2:
time: 496 us; the launch traced here: 489 us
  waiting for transfers between devices  268 us (54%)
  Pallas kernels  59.8 us (12%)
  starting transfers between devices  58.7 us (12%)
  other arithmetic  46.9 us (9%)
  matrix products  43.3 us (9%)
  local copies, waits for them, and re-layouts  10.9 us (2%)
    ppermute x7, waiting for transfers between devices, shards(): weight = lax.ppermute(weight, 'dp', turn)  179 us
    ppermute x6, waiting for transfers between devices, shards(): halos.append((lax.ppermute(pair, 'dp', up), lax.ppermute(pair, 'dp', down)))  59.2 us
    pallas_call x3, Pallas kernels, attend(): pl.pallas_call(functools.partial(attend_kernel, heads=heads, rows=rows),...  48 us
    dot_general x8, matrix products, shards(): partial_value = jnp.dot(both, weight, preferred_element_type=jnp.float32)  43.3 us
    concatenate x1, other arithmetic, shards(): jnp.concatenate([jnp.concatenate(own, axis=1), jnp.concatenate(other, axi...  33 us
    ppermute x8, waiting for transfers between devices, shards(): lax.ppermute(away, 'mp', [(i, (i + k) % groups) for i in range(groups)])  30.5 us
    ppermute x7, starting transfers between devices, shards(): weight = lax.ppermute(weight, 'dp', turn)  22.7 us
    ppermute x6, starting transfers between devices, shards(): halos.append((lax.ppermute(pair, 'dp', up), lax.ppermute(pair, 'dp', down)))  18.3 us
  transfers between devices with their start and end apart: 26, of which 12 were waited for; matrix products, arithmetic and copies ran while one was open for 18% of the time, Pallas kernels for 10%

profile of v2, /device:TPU:1, one launch (start us, length us, event | category | flops | bytes accessed | tf_op | source)
XLA Modules:
  0.0 488.5 jit_solution(9011866398307040762)
XLA Ops:
  0.0 4.3 fusion.16
  6.3 4.5 collective-permute-start
  16.1 3.6 collective-permute-start.2
  24.0 113.9 %collective-permute-done.10 = bf16[3072,384]{1,0:T(8,128)(2,1)S(1)} collective-permute-done((bf16[3072,384]{1,0:T(8,128)(2,1)S(1)}, bf16[3072,384]{1,0:T(8,128)(2,1)S(1)}, u32[]{:S(2)}, u32[]{:S(2)}) %collective-permute-start.10) | collective-permute-done | bytes 2359328 | tf_op jit(solution)/shard_map/ppermute | solution.py:141
  139.9 4.0 collective-permute-start.5
  147.8 16.3 %shard_map.64 = bf16[768,1024]{1,0:T(8,128)(2,1)} custom-call(s32[2,3]{1,0:T(2,128)S(1)} %pad_add_fusion.span_ref, bf16[768,3072]{1,0:T(8,128)(2,1)S(1)} %copy-done, bf16[768,2048]{1,0:T(8,128)(2,1)S(1)} %collective-permute-done.kb_ref.vb_ref, bf16[768,3072]{1,0:T(8,128)(2,1)} %k_ref.5, bf16[768,2048]{1,0:T(8,128)(2,1)} %collective-permute-done.1.ka_ref.va_ref, ...), custom_call_target="tpu_custom_call" | custom-call | flops 2415919104 | bytes 12582912 | tf_op jit(solution)/shard_map/pallas_call | solution.py:71
  164.0 41.4 %collective-permute-done.2.kb_ref.vb_ref = bf16[768,2048]{1,0:T(8,128)(2,1)} collective-permute-done((bf16[768,2048]{1,0:T(8,128)(2,1)}, bf16[768,2048]{1,0:T(8,128)(2,1)}, u32[]{:S(2)}, u32[]{:S(2)}) %collective-permute-start.2) | collective-permute-done | bytes 3145760 | tf_op jit(solution)/shard_map/ppermute | solution.py:103
  205.5 15.9 %shard_map.65 = bf16[768,1024]{1,0:T(8,128)(2,1)S(1)} custom-call(s32[2,3]{1,0:T(2,128)S(1)} %pad_add_fusion.span_ref, bf16[768,3072]{1,0:T(8,128)(2,1)S(1)} %copy-done, bf16[768,2048]{1,0:T(8,128)(2,1)} %collective-permute-done.2.kb_ref.vb_ref, bf16[768,3072]{1,0:T(8,128)(2,1)} %k_ref.5, bf16[768,2048]{1,0:T(8,128)(2,1)} %collective-permute-done.3.ka_ref.va_ref, ...), custom_call_target="tpu_custom_call" | custom-call | flops 2415919104 | bytes 12582912 | tf_op jit(solution)/shard_map/pallas_call | solution.py:71
  221.4 17.7 %collective-permute-done.4.kb_ref.vb_ref = bf16[768,2048]{1,0:T(8,128)(2,1)} collective-permute-done((bf16[768,2048]{1,0:T(8,128)(2,1)}, bf16[768,2048]{1,0:T(8,128)(2,1)}, u32[]{:S(2)}, u32[]{:S(2)}) %collective-permute-start.4) | collective-permute-done | bytes 3145760 | tf_op jit(solution)/shard_map/ppermute | solution.py:103
  239.2 15.9 %shard_map.66 = bf16[768,1024]{1,0:T(8,128)(2,1)S(1)} custom-call(s32[2,3]{1,0:T(2,128)S(1)} %pad_add_fusion.span_ref, bf16[768,3072]{1,0:T(8,128)(2,1)S(1)} %copy-done, bf16[768,2048]{1,0:T(8,128)(2,1)} %collective-permute-done.4.kb_ref.vb_ref, bf16[768,3072]{1,0:T(8,128)(2,1)} %k_ref.5, bf16[768,2048]{1,0:T(8,128)(2,1)} %collective-permute-done.5.ka_ref.va_ref, ...), custom_call_target="tpu_custom_call" | custom-call | flops 2415919104 | bytes 12582912 | tf_op jit(solution)/shard_map/pallas_call | solution.py:71
  255.2 9.3 %collective-permute-done.12 = bf16[3072,384]{1,0:T(8,128)(2,1)} collective-permute-done((bf16[3072,384]{1,0:T(8,128)(2,1)}, bf16[3072,384]{1,0:T(8,128)(2,1)}, u32[]{:S(2)}, u32[]{:S(2)}) %collective-permute-start.12) | collective-permute-done | bytes 2359328 | tf_op jit(solution)/shard_map/ppermute | solution.py:141
  267.0 33.0 %maximum_maximum_fusion = bf16[1536,3072]{1,0:T(8,128)(2,1)S(1)} fusion(bf16[768,1024]{1,0:T(8,128)(2,1)} %collective-permute-done.8, bf16[768,1024]{1,0:T(8,128)(2,1)} %collective-permute-done.7, bf16[768,1024]{1,0:T(8,128)(2,1)} %collective-permute-done.6, bf16[768,1024]{1,0:T(8,128)(2,1)S(1)} %shard_map.66, bf16[768,1024]{1,0:T(8,128)(2,1)S(1)} %shard_map.65, ...), kind=kLoop, calls=%fused_computation.1 | loop fusion | flops 56623104 | bytes 18874368 | tf_op jit(solution)/shard_map/concatenate | solution.py:135
  300.0 5.2 %convolution_convert_fusion.7 = bf16[1536,384]{1,0:T(8,128)(2,1)S(1)} fusion(bf16[1536,3072]{1,0:T(8,128)(2,1)S(1)} %maximum_maximum_fusion, bf16[3072,384]{1,0:T(8,128)(2,1)S(1)} %copy-done.5), kind=kOutput, calls=%fused_computation.12 | convolution fusion | flops 3624468480 | bytes 12976128 | tf_op jit(solution)/shard_map/dot_general | solution.py:142
  306.6 5.2 %convolution_convert_fusion.6 = bf16[1536,384]{1,0:T(8,128)(2,1)S(1)} fusion(bf16[1536,3072]{1,0:T(8,128)(2,1)S(1)} %maximum_maximum_fusion, bf16[3072,384]{1,0:T(8,128)(2,1)S(1)} %copy-done.7), kind=kOutput, calls=%fused_computation.11 | convolution fusion | flops 3624468480 | bytes 12976128 | tf_op jit(solution)/shard_map/dot_general | solution.py:142
  312.4 6.8 %convolution_convert_fusion.5 = bf16[1536,384]{1,0:T(8,128)(2,1)S(1)} fusion(bf16[1536,3072]{1,0:T(8,128)(2,1)S(1)} %maximum_maximum_fusion, bf16[3072,384]{1,0:T(8,128)(2,1)} %collective-permute-done.12), kind=kOutput, calls=%fused_computation.10 | convolution fusion | flops 3624468480 | bytes 12976128 | tf_op jit(solution)/shard_map/dot_general | solution.py:142
  320.9 11.5 %collective-permute-done.11 = bf16[2,384,384]{2,1,0:T(8,128)(2,1)S(1)} collective-permute-done((bf16[2,384,384]{2,1,0:T(8,128)(2,1)S(1)}, bf16[2,384,384]{2,1,0:T(8,128)(2,1)S(1)}, u32[]{:S(2)}, u32[]{:S(2)}) %collective-permute-start.11) | collective-permute-done | bytes 589856 | tf_op jit(solution)/shard_map/ppermute | solution.py:147
  332.6 7.8 %collective-permute-done.16 = bf16[3072,384]{1,0:T(8,128)(2,1)S(1)} collective-permute-done((bf16[3072,384]{1,0:T(8,128)(2,1)S(1)}, bf16[3072,384]{1,0:T(8,128)(2,1)S(1)}, u32[]{:S(2)}, u32[]{:S(2)}) %collective-permute-start.16) | collective-permute-done | bytes 2359328 | tf_op jit(solution)/shard_map/ppermute | solution.py:141
  340.4 5.2 %convolution_convert_fusion.4 = bf16[1536,384]{1,0:T(8,128)(2,1)S(1)} fusion(bf16[1536,3072]{1,0:T(8,128)(2,1)S(1)} %maximum_maximum_fusion, bf16[3072,384]{1,0:T(8,128)(2,1)S(1)} %collective-permute-done.14), kind=kOutput, calls=%fused_computation.9 | convolution fusion | flops 3624468480 | bytes 12976128 | tf_op jit(solution)/shard_map/dot_general | solution.py:142
  347.3 7.5 %collective-permute-done.15 = bf16[2,384,384]{2,1,0:T(8,128)(2,1)S(1)} collective-permute-done((bf16[2,384,384]{2,1,0:T(8,128)(2,1)S(1)}, bf16[2,384,384]{2,1,0:T(8,128)(2,1)S(1)}, u32[]{:S(2)}, u32[]{:S(2)}) %collective-permute-start.15) | collective-permute-done | bytes 589856 | tf_op jit(solution)/shard_map/ppermute | solution.py:147
  355.0 14.4 %collective-permute-done.18 = bf16[3072,384]{1,0:T(8,128)(2,1)S(1)} collective-permute-done((bf16[3072,384]{1,0:T(8,128)(2,1)S(1)}, bf16[3072,384]{1,0:T(8,128)(2,1)S(1)}, u32[]{:S(2)}, u32[]{:S(2)}) %collective-permute-start.18) | collective-permute-done | bytes 2359328 | tf_op jit(solution)/shard_map/ppermute | solution.py:141
  369.4 18.1 %collective-permute-start.20 = (bf16[3072,384]{1,0:T(8,128)(2,1)S(1)}, bf16[3072,384]{1,0:T(8,128)(2,1)S(1)}, u32[]{:S(2)}, u32[]{:S(2)}) collective-permute-start(bf16[3072,384]{1,0:T(8,128)(2,1)S(1)} %collective-permute-done.18), channel_id=1, source_target_pairs={{0,8},{8,16},{16,24},{24,28},{28,20},{20,12},{12,4},{4,0},{10,2},{... | collective-permute-start | bytes 7077896 | tf_op jit(solution)/shard_map/ppermute | solution.py:141
  387.5 5.2 %convolution_convert_fusion.3 = bf16[1536,384]{1,0:T(8,128)(2,1)S(1)} fusion(bf16[1536,3072]{1,0:T(8,128)(2,1)S(1)} %maximum_maximum_fusion, bf16[3072,384]{1,0:T(8,128)(2,1)S(1)} %collective-permute-done.16), kind=kOutput, calls=%fused_computation.8 | convolution fusion | flops 3624468480 | bytes 12976128 | tf_op jit(solution)/shard_map/dot_general | solution.py:142
  394.1 5.2 %convolution_convert_fusion.2 = bf16[1536,384]{1,0:T(8,128)(2,1)S(1)} fusion(bf16[1536,3072]{1,0:T(8,128)(2,1)S(1)} %maximum_maximum_fusion, bf16[3072,384]{1,0:T(8,128)(2,1)S(1)} %collective-permute-done.18), kind=kOutput, calls=%fused_computation.7 | convolution fusion | flops 3624468480 | bytes 12976128 | tf_op jit(solution)/shard_map/dot_general | solution.py:142
  399.9 6.5 %collective-permute-start.24 = (bf16[4,384,384]{2,1,0:T(8,128)(2,1)S(1)}, bf16[4,384,384]{2,1,0:T(8,128)(2,1)}, u32[]{:S(2)}, u32[]{:S(2)}) collective-permute-start(bf16[4,384,384]{2,1,0:T(8,128)(2,1)S(1)} %pad_maximum_fusion.4), channel_id=1, source_target_pairs={{0,2},{2,0},{4,6},{6,4},{8,10},{10,8},{12,14},{14,12},{16,18},{18,... | collective-permute-start | bytes 3538952 | tf_op jit(solution)/shard_map/ppermute | solution.py:153
  406.3 12.3 %collective-permute-done.20 = bf16[3072,384]{1,0:T(8,128)(2,1)S(1)} collective-permute-done((bf16[3072,384]{1,0:T(8,128)(2,1)S(1)}, bf16[3072,384]{1,0:T(8,128)(2,1)S(1)}, u32[]{:S(2)}, u32[]{:S(2)}) %collective-permute-start.20) | collective-permute-done | bytes 2359328 | tf_op jit(solution)/shard_map/ppermute | solution.py:141
  419.2 5.2 %convolution_convert_fusion.1 = bf16[1536,384]{1,0:T(8,128)(2,1)S(1)} fusion(bf16[1536,3072]{1,0:T(8,128)(2,1)S(1)} %maximum_maximum_fusion, bf16[3072,384]{1,0:T(8,128)(2,1)S(1)} %collective-permute-done.20), kind=kOutput, calls=%fused_computation.6 | convolution fusion | flops 3624468480 | bytes 12976128 | tf_op jit(solution)/shard_map/dot_general | solution.py:142
  425.8 21.0 %collective-permute-done.22 = bf16[3072,384]{1,0:T(8,128)(2,1)S(1)} collective-permute-done((bf16[3072,384]{1,0:T(8,128)(2,1)S(1)}, bf16[3072,384]{1,0:T(8,128)(2,1)S(1)}, u32[]{:S(2)}, u32[]{:S(2)}) %collective-permute-start.22) | collective-permute-done | bytes 2359328 | tf_op jit(solution)/shard_map/ppermute | solution.py:141
  446.8 5.2 %convolution_convert_fusion = bf16[1536,384]{1,0:T(8,128)(2,1)S(1)} fusion(bf16[1536,3072]{1,0:T(8,128)(2,1)S(1)} %maximum_maximum_fusion, bf16[3072,384]{1,0:T(8,128)(2,1)S(1)} %collective-permute-done.22), kind=kOutput, calls=%fused_computation.5 | convolution fusion | flops 3624468480 | bytes 12976128 | tf_op jit(solution)/shard_map/dot_general | solution.py:142
  453.7 11.4 %collective-permute-done.23 = bf16[2,384,384]{2,1,0:T(8,128)(2,1)S(1)} collective-permute-done((bf16[2,384,384]{2,1,0:T(8,128)(2,1)S(1)}, bf16[2,384,384]{2,1,0:T(8,128)(2,1)S(1)}, u32[]{:S(2)}, u32[]{:S(2)}) %collective-permute-start.23) | collective-permute-done | bytes 589856 | tf_op jit(solution)/shard_map/ppermute | solution.py:147
  466.7 2.8 collective-permute-start.25
  473.2 3.3 pad_maximum_fusion.3.theirs_ref
  476.6 11.7 %shard_map.67 = bf16[384,6144]{1,0:T(8,128)(2,1)} custom-call(s32[16]{0:T(128)} %reshape.302.mine_at, s32[16]{0:T(128)} %reshape.303.theirs_at, s32[1]{0:T(128)} %bitcast.2.core_ref, bf16[8,384,384]{2,1,0:T(8,128)(2,1)} %copy-done.2, bf16[8,384,384]{2,1,0:T(8,128)(2,1)} %pad_maximum_fusion.3.theirs_ref), custom_call_target="tpu_custom_call" | custom-call | bytes 9437184 | tf_op jit(solution)/shard_map/pallas_call | solution.py:190
  (110 shorter events, 36.4 us)
Async XLA Ops:
  4.3 6.6 %copy-start.4 = (bf16[3072,384]{1,0:T(8,128)(2,1)S(1)}, bf16[3072,384]{1,0:T(8,128)(2,1)}, u32[]{:S(2)}) copy-start(bf16[3072,384]{1,0:T(8,128)(2,1)} %param.10) | copy-start | bytes 7077892
  6.3 133.6 %collective-permute-start = (bf16[768,2048]{1,0:T(8,128)(2,1)}, bf16[768,2048]{1,0:T(8,128)(2,1)S(1)}, u32[]{:S(2)}, u32[]{:S(2)}) collective-permute-start(bf16[768,2048]{1,0:T(8,128)(2,1)} %pad_maximum_fusion), channel_id=1, source_target_pairs={{0,2},{2,4},{4,6},{6,8},{8,10},{10,12},{12,14},{14,16},{16,18},{18... | collective-permute-start | bytes 9437192 | tf_op jit(solution)/shard_map/ppermute | solution.py:103
  10.8 127.1 %collective-permute-start.10 = (bf16[3072,384]{1,0:T(8,128)(2,1)S(1)}, bf16[3072,384]{1,0:T(8,128)(2,1)S(1)}, u32[]{:S(2)}, u32[]{:S(2)}) collective-permute-start(bf16[3072,384]{1,0:T(8,128)(2,1)S(1)} %copy-done.4), channel_id=1, source_target_pairs={{0,8},{8,16},{16,24},{24,28},{28,20},{20,12},{12,4},{4,0},{10,2},{... | collective-permute-start | bytes 7077896 | tf_op jit(solution)/shard_map/ppermute | solution.py:141
  12.1 132.7 %collective-permute-start.1 = (bf16[768,2048]{1,0:T(8,128)(2,1)}, bf16[768,2048]{1,0:T(8,128)(2,1)}, u32[]{:S(2)}, u32[]{:S(2)}) collective-permute-start(bf16[768,2048]{1,0:T(8,128)(2,1)} %pad_maximum_fusion), channel_id=1, source_target_pairs={{2,0},{4,2},{6,4},{8,6},{10,8},{12,10},{14,12},{16,14},{18,16},{20... | collective-permute-start | bytes 9437192 | tf_op jit(solution)/shard_map/ppermute | solution.py:103
  16.1 189.4 %collective-permute-start.2 = (bf16[768,2048]{1,0:T(8,128)(2,1)}, bf16[768,2048]{1,0:T(8,128)(2,1)}, u32[]{:S(2)}, u32[]{:S(2)}) collective-permute-start(bf16[768,2048]{1,0:T(8,128)(2,1)} %pad_maximum_fusion.1), channel_id=1, source_target_pairs={{0,2},{2,4},{4,6},{6,8},{8,10},{10,12},{12,14},{14,16},{16,18},{18... | collective-permute-start | bytes 9437192 | tf_op jit(solution)/shard_map/ppermute | solution.py:103
  19.7 185.8 %collective-permute-start.3 = (bf16[768,2048]{1,0:T(8,128)(2,1)}, bf16[768,2048]{1,0:T(8,128)(2,1)}, u32[]{:S(2)}, u32[]{:S(2)}) collective-permute-start(bf16[768,2048]{1,0:T(8,128)(2,1)} %pad_maximum_fusion.1), channel_id=1, source_target_pairs={{2,0},{4,2},{6,4},{8,6},{10,8},{12,10},{14,12},{16,14},{18,16},{20... | collective-permute-start | bytes 9437192 | tf_op jit(solution)/shard_map/ppermute | solution.py:103
  22.1 121.8 %copy-start.3 = (s32[64]{0:T(128)S(1)}, s32[64]{0:T(128)}, u32[]{:S(2)}) copy-start(s32[64]{0:T(128)} %param.9) | copy-start | bytes 772
  137.9 101.2 %collective-permute-start.4 = (bf16[768,2048]{1,0:T(8,128)(2,1)}, bf16[768,2048]{1,0:T(8,128)(2,1)}, u32[]{:S(2)}, u32[]{:S(2)}) collective-permute-start(bf16[768,2048]{1,0:T(8,128)(2,1)} %pad_maximum_fusion.2), channel_id=1, source_target_pairs={{0,2},{2,4},{4,6},{6,8},{8,10},{10,12},{12,14},{14,16},{16,18},{18... | collective-permute-start | bytes 9437192 | tf_op jit(solution)/shard_map/ppermute | solution.py:103
  139.9 99.3 %collective-permute-start.5 = (bf16[768,2048]{1,0:T(8,128)(2,1)}, bf16[768,2048]{1,0:T(8,128)(2,1)}, u32[]{:S(2)}, u32[]{:S(2)}) collective-permute-start(bf16[768,2048]{1,0:T(8,128)(2,1)} %pad_maximum_fusion.2), channel_id=1, source_target_pairs={{2,0},{4,2},{6,4},{8,6},{10,8},{12,10},{14,12},{16,14},{18,16},{20... | collective-permute-start | bytes 9437192 | tf_op jit(solution)/shard_map/ppermute | solution.py:103
  144.9 119.5 %collective-permute-start.12 = (bf16[3072,384]{1,0:T(8,128)(2,1)}, bf16[3072,384]{1,0:T(8,128)(2,1)}, u32[]{:S(2)}, u32[]{:S(2)}) collective-permute-start(bf16[3072,384]{1,0:T(8,128)(2,1)} %copy-done.6), channel_id=1, source_target_pairs={{0,8},{8,16},{16,24},{24,28},{28,20},{20,12},{12,4},{4,0},{10,2},{... | collective-permute-start | bytes 7077896 | tf_op jit(solution)/shard_map/ppermute | solution.py:141
  205.5 61.5 %collective-permute-start.6 = (bf16[768,1024]{1,0:T(8,128)(2,1)}, bf16[768,1024]{1,0:T(8,128)(2,1)}, u32[]{:S(2)}, u32[]{:S(2)}) collective-permute-start(bf16[768,1024]{1,0:T(8,128)(2,1)} %shard_map.64), channel_id=1, source_target_pairs={{0,2},{2,0},{4,6},{6,4},{8,10},{10,8},{12,14},{14,12},{16,18},{18,... | collective-permute-start | bytes 4718600 | tf_op jit(solution)/shard_map/ppermute | solution.py:134
  221.4 45.6 %collective-permute-start.7 = (bf16[768,1024]{1,0:T(8,128)(2,1)S(1)}, bf16[768,1024]{1,0:T(8,128)(2,1)}, u32[]{:S(2)}, u32[]{:S(2)}) collective-permute-start(bf16[768,1024]{1,0:T(8,128)(2,1)S(1)} %shard_map.65), channel_id=1, source_target_pairs={{0,2},{2,0},{4,6},{6,4},{8,10},{10,8},{12,14},{14,12},{16,18},{18,... | collective-permute-start | bytes 4718600 | tf_op jit(solution)/shard_map/ppermute | solution.py:134
  255.0 11.9 %collective-permute-start.8 = (bf16[768,1024]{1,0:T(8,128)(2,1)S(1)}, bf16[768,1024]{1,0:T(8,128)(2,1)}, u32[]{:S(2)}, u32[]{:S(2)}) collective-permute-start(bf16[768,1024]{1,0:T(8,128)(2,1)S(1)} %shard_map.66), channel_id=1, source_target_pairs={{0,2},{2,0},{4,6},{6,4},{8,10},{10,8},{12,14},{14,12},{16,18},{18,... | collective-permute-start | bytes 4718600 | tf_op jit(solution)/shard_map/ppermute | solution.py:134
  255.1 44.9 %copy-start.5 = (bf16[3072,384]{1,0:T(8,128)(2,1)S(1)}, bf16[3072,384]{1,0:T(8,128)(2,1)}, u32[]{:S(2)}) copy-start(bf16[3072,384]{1,0:T(8,128)(2,1)} %param.10) | copy-start | bytes 7077892
  264.4 47.8 %collective-permute-start.14 = (bf16[3072,384]{1,0:T(8,128)(2,1)}, bf16[3072,384]{1,0:T(8,128)(2,1)S(1)}, u32[]{:S(2)}, u32[]{:S(2)}) collective-permute-start(bf16[3072,384]{1,0:T(8,128)(2,1)} %collective-permute-done.12), channel_id=1, source_target_pairs={{0,8},{8,16},{16,24},{24,28},{28,20},{20,12},{12,4},{4,0},{10,2},{... | collective-permute-start | bytes 7077896 | tf_op jit(solution)/shard_map/ppermute | solution.py:141
  300.0 6.6 %copy-start.7 = (bf16[3072,384]{1,0:T(8,128)(2,1)S(1)}, bf16[3072,384]{1,0:T(8,128)(2,1)}, u32[]{:S(2)}) copy-start(bf16[3072,384]{1,0:T(8,128)(2,1)} %copy-done.6) | copy-start | bytes 7077892
  305.3 15.4 %collective-permute-start.9 = (bf16[2,384,384]{2,1,0:T(8,128)(2,1)S(1)}, bf16[2,384,384]{2,1,0:T(8,128)(2,1)S(1)}, u32[]{:S(2)}, u32[]{:S(2)}) collective-permute-start(bf16[2,384,384]{2,1,0:T(8,128)(2,1)S(1)} %dynamic-slice_bitcast_fusion.7), channel_id=1, source_target_pairs={{0,1},{1,0},{2,3},{3,2},{4,5},{5,4},{6,7},{7,6},{8,9},{9,8},{10,11... | collective-permute-start | bytes 1769480 | tf_op jit(solution)/shard_map/ppermute | solution.py:147
  311.9 20.6 %collective-permute-start.11 = (bf16[2,384,384]{2,1,0:T(8,128)(2,1)S(1)}, bf16[2,384,384]{2,1,0:T(8,128)(2,1)S(1)}, u32[]{:S(2)}, u32[]{:S(2)}) collective-permute-start(bf16[2,384,384]{2,1,0:T(8,128)(2,1)S(1)} %dynamic-slice_bitcast_fusion.6), channel_id=1, source_target_pairs={{0,1},{1,0},{2,3},{3,2},{4,5},{5,4},{6,7},{7,6},{8,9},{9,8},{10,11... | collective-permute-start | bytes 1769480 | tf_op jit(solution)/shard_map/ppermute | solution.py:147
  312.2 28.2 %collective-permute-start.16 = (bf16[3072,384]{1,0:T(8,128)(2,1)S(1)}, bf16[3072,384]{1,0:T(8,128)(2,1)S(1)}, u32[]{:S(2)}, u32[]{:S(2)}) collective-permute-start(bf16[3072,384]{1,0:T(8,128)(2,1)S(1)} %collective-permute-done.14), channel_id=1, source_target_pairs={{0,8},{8,16},{16,24},{24,28},{28,20},{20,12},{12,4},{4,0},{10,2},{... | collective-permute-start | bytes 7077896 | tf_op jit(solution)/shard_map/ppermute | solution.py:141
  319.3 27.7 %collective-permute-start.13 = (bf16[2,384,384]{2,1,0:T(8,128)(2,1)S(1)}, bf16[2,384,384]{2,1,0:T(8,128)(2,1)S(1)}, u32[]{:S(2)}, u32[]{:S(2)}) collective-permute-start(bf16[2,384,384]{2,1,0:T(8,128)(2,1)S(1)} %dynamic-slice_bitcast_fusion.5), channel_id=1, source_target_pairs={{0,1},{1,0},{2,3},{3,2},{4,5},{5,4},{6,7},{7,6},{8,9},{9,8},{10,11... | collective-permute-start | bytes 1769480 | tf_op jit(solution)/shard_map/ppermute | solution.py:147
  340.4 29.0 %collective-permute-start.18 = (bf16[3072,384]{1,0:T(8,128)(2,1)S(1)}, bf16[3072,384]{1,0:T(8,128)(2,1)S(1)}, u32[]{:S(2)}, u32[]{:S(2)}) collective-permute-start(bf16[3072,384]{1,0:T(8,128)(2,1)S(1)} %collective-permute-done.16), channel_id=1, source_target_pairs={{0,8},{8,16},{16,24},{24,28},{28,20},{20,12},{12,4},{4,0},{10,2},{... | collective-permute-start | bytes 7077896 | tf_op jit(solution)/shard_map/ppermute | solution.py:141
  345.7 9.1 %collective-permute-start.15 = (bf16[2,384,384]{2,1,0:T(8,128)(2,1)S(1)}, bf16[2,384,384]{2,1,0:T(8,128)(2,1)S(1)}, u32[]{:S(2)}, u32[]{:S(2)}) collective-permute-start(bf16[2,384,384]{2,1,0:T(8,128)(2,1)S(1)} %dynamic-slice_bitcast_fusion.4), channel_id=1, source_target_pairs={{0,1},{1,0},{2,3},{3,2},{4,5},{5,4},{6,7},{7,6},{8,9},{9,8},{10,11... | collective-permute-start | bytes 1769480 | tf_op jit(solution)/shard_map/ppermute | solution.py:147
  369.4 49.2 %collective-permute-start.20 = (bf16[3072,384]{1,0:T(8,128)(2,1)S(1)}, bf16[3072,384]{1,0:T(8,128)(2,1)S(1)}, u32[]{:S(2)}, u32[]{:S(2)}) collective-permute-start(bf16[3072,384]{1,0:T(8,128)(2,1)S(1)} %collective-permute-done.18), channel_id=1, source_target_pairs={{0,8},{8,16},{16,24},{24,28},{28,20},{20,12},{12,4},{4,0},{10,2},{... | collective-permute-start | bytes 7077896 | tf_op jit(solution)/shard_map/ppermute | solution.py:141
  392.8 26.0 %collective-permute-start.17 = (bf16[2,384,384]{2,1,0:T(8,128)(2,1)S(1)}, bf16[2,384,384]{2,1,0:T(8,128)(2,1)S(1)}, u32[]{:S(2)}, u32[]{:S(2)}) collective-permute-start(bf16[2,384,384]{2,1,0:T(8,128)(2,1)S(1)} %dynamic-slice_bitcast_fusion.3), channel_id=1, source_target_pairs={{0,1},{1,0},{2,3},{3,2},{4,5},{5,4},{6,7},{7,6},{8,9},{9,8},{10,11... | collective-permute-start | bytes 1769480 | tf_op jit(solution)/shard_map/ppermute | solution.py:147
  399.3 19.7 %collective-permute-start.19 = (bf16[2,384,384]{2,1,0:T(8,128)(2,1)S(1)}, bf16[2,384,384]{2,1,0:T(8,128)(2,1)S(1)}, u32[]{:S(2)}, u32[]{:S(2)}) collective-permute-start(bf16[2,384,384]{2,1,0:T(8,128)(2,1)S(1)} %dynamic-slice_bitcast_fusion.2), channel_id=1, source_target_pairs={{0,1},{1,0},{2,3},{3,2},{4,5},{5,4},{6,7},{7,6},{8,9},{9,8},{10,11... | collective-permute-start | bytes 1769480 | tf_op jit(solution)/shard_map/ppermute | solution.py:147
  399.9 73.4 %collective-permute-start.24 = (bf16[4,384,384]{2,1,0:T(8,128)(2,1)S(1)}, bf16[4,384,384]{2,1,0:T(8,128)(2,1)}, u32[]{:S(2)}, u32[]{:S(2)}) collective-permute-start(bf16[4,384,384]{2,1,0:T(8,128)(2,1)S(1)} %pad_maximum_fusion.4), channel_id=1, source_target_pairs={{0,2},{2,0},{4,6},{6,4},{8,10},{10,8},{12,14},{14,12},{16,18},{18,... | collective-permute-start | bytes 3538952 | tf_op jit(solution)/shard_map/ppermute | solution.py:153
  418.6 28.1 %collective-permute-start.22 = (bf16[3072,384]{1,0:T(8,128)(2,1)S(1)}, bf16[3072,384]{1,0:T(8,128)(2,1)S(1)}, u32[]{:S(2)}, u32[]{:S(2)}) collective-permute-start(bf16[3072,384]{1,0:T(8,128)(2,1)S(1)} %collective-permute-done.20), channel_id=1, source_target_pairs={{0,8},{8,16},{16,24},{24,28},{28,20},{20,12},{12,4},{4,0},{10,2},{... | collective-permute-start | bytes 7077896 | tf_op jit(solution)/shard_map/ppermute | solution.py:141
  424.5 28.9 %collective-permute-start.21 = (bf16[2,384,384]{2,1,0:T(8,128)(2,1)S(1)}, bf16[2,384,384]{2,1,0:T(8,128)(2,1)S(1)}, u32[]{:S(2)}, u32[]{:S(2)}) collective-permute-start(bf16[2,384,384]{2,1,0:T(8,128)(2,1)S(1)} %dynamic-slice_bitcast_fusion.1), channel_id=1, source_target_pairs={{0,1},{1,0},{2,3},{3,2},{4,5},{5,4},{6,7},{7,6},{8,9},{9,8},{10,11... | collective-permute-start | bytes 1769480 | tf_op jit(solution)/shard_map/ppermute | solution.py:147
  452.1 13.0 %collective-permute-start.23 = (bf16[2,384,384]{2,1,0:T(8,128)(2,1)S(1)}, bf16[2,384,384]{2,1,0:T(8,128)(2,1)S(1)}, u32[]{:S(2)}, u32[]{:S(2)}) collective-permute-start(bf16[2,384,384]{2,1,0:T(8,128)(2,1)S(1)} %dynamic-slice_bitcast_fusion), channel_id=1, source_target_pairs={{0,1},{1,0},{2,3},{3,2},{4,5},{5,4},{6,7},{7,6},{8,9},{9,8},{10,11... | collective-permute-start | bytes 1769480 | tf_op jit(solution)/shard_map/ppermute | solution.py:147
  453.7 15.8 %copy-start.1 = (s32[8]{0:T(128)S(1)}, s32[8]{0:T(128)}, u32[]{:S(2)}) copy-start(s32[8]{0:T(128)} %constant.180.clone) | copy-start | bytes 100
  465.3 11.3 %copy-start.2 = (bf16[8,384,384]{2,1,0:T(8,128)(2,1)}, bf16[8,384,384]{2,1,0:T(8,128)(2,1)S(1)}, u32[]{:S(2)}) copy-start(bf16[8,384,384]{2,1,0:T(8,128)(2,1)S(1)} %get-tuple-element.28.mine_ref) | copy-start | bytes 7077892
  466.7 6.6 %collective-permute-start.25 = (bf16[4,384,384]{2,1,0:T(8,128)(2,1)}, bf16[4,384,384]{2,1,0:T(8,128)(2,1)}, u32[]{:S(2)}, u32[]{:S(2)}) collective-permute-start(bf16[4,384,384]{2,1,0:T(8,128)(2,1)} %pad_maximum_fusion.5), channel_id=1, source_target_pairs={{0,2},{2,0},{4,6},{6,4},{8,10},{10,8},{12,14},{14,12},{16,18},{18,... | collective-permute-start | bytes 3538952 | tf_op jit(solution)/shard_map/ppermute | solution.py:153
  (2 other events, 4.3 us)

commit v3 on v2

--- a/solution.py
+++ b/solution.py
@@ -10,7 +10,7 @@
 HEAD_DIM = 128
 Q_ROWS = 256
 K_ROWS = 256
-CHUNKS = 3
+CHUNKS = 2
 LOG2E = 1.4426950408889634
 
 
@@ -82,7 +82,7 @@
         ),
         out_shape=jax.ShapeDtypeStruct((rows, width), jnp.bfloat16),
         compiler_params=pltpu.CompilerParams(vmem_limit_bytes=40 * 2 ** 20),
-        cost_estimate=pl.CostEstimate(flops=4 * rows * rows * width, bytes_accessed=16 * rows * width,
+        cost_estimate=pl.CostEstimate(flops=32 * rows * rows * width, bytes_accessed=16 * rows * width,
                                       transcendentals=rows * rows * width // HEAD_DIM),
     )(span, queries, before, keys, after, before, values, after, q_seg, k_seg)
 
@@ -98,8 +98,6 @@
     for c in range(CHUNKS):
         at = slice(c * width, (c + 1) * width)
         pair = jnp.concatenate([keys[:, at], values[:, at]], axis=1)
-        if halos:
-            pair, _ = lax.optimization_barrier((pair, halos[-1][0][:8, :128]))
         halos.append((lax.ppermute(pair, "dp", up), lax.ppermute(pair, "dp", down)))
 
     row_first = lax.axis_index("dp") * rows
@@ -128,18 +126,20 @@
     block = rows // groups
     me = lax.axis_index("mp")
 
-    own, other = [], []
+    weights = [out_weight]
+    for step in range(1, chips):
+        weights.append(lax.ppermute(weights[-1], "dp", turn))
+    both = jnp.zeros((2, rows, columns), jnp.bfloat16)
     for c in range(CHUNKS):
-        own.append(attend(span, queries, keys, values, *halos[c], q_seg, k_seg, c, width))
-        other.append(lax.ppermute(own[-1], "dp", swap))
-    both = jnp.concatenate([jnp.concatenate(own, axis=1), jnp.concatenate(other, axis=1)], axis=0)
-
-    weight = out_weight
+        own = attend(span, queries, keys, values, *halos[c], q_seg, k_seg, c, width)
+        other = lax.ppermute(own, "dp", swap)
+        both = lax.dynamic_update_slice(both, own[None], (0, 0, c * width))
+        both = lax.dynamic_update_slice(both, other[None], (1, 0, c * width))
+    both = both.reshape(2 * rows, columns)
+
     mine, theirs, batch = [], [], []
     for step in range(chips):
-        if step:
-            weight = lax.ppermute(weight, "dp", turn)
-        partial_value = jnp.dot(both, weight, preferred_element_type=jnp.float32)
+        partial_value = jnp.dot(both, weights[step], preferred_element_type=jnp.float32)
         partial_value = partial_value.astype(jnp.bfloat16).reshape(2, groups, block, part)
         total = lax.dynamic_index_in_dim(partial_value, me, 1, False).astype(jnp.float32)
         for k in range(1, groups):
@@ -152,7 +152,7 @@
         if step % (chips // 2) == chips // 2 - 1:
             theirs.append(lax.ppermute(jnp.stack(batch), "dp", swap))
             batch = []
-    mine, theirs = jnp.stack(mine), jnp.concatenate(theirs, axis=0)
+    mine = jnp.stack(mine)
 
     place = jnp.array([ring.index(c) for c in range(chips)], jnp.int32)
     index = lax.axis_index("dp")
@@ -161,44 +161,52 @@
     ahead = (at - place[owner // 2]) % chips
     behind = (place[owner // 2] - at) % chips
     step_of = jnp.where(owner % 2 == 0, ahead, behind)
-    return assemble(mine, theirs, step_of, core)
-
-
-def assemble_kernel(mine_at, theirs_at, core_ref, mine_ref, theirs_ref, out_ref):
-    is_mine = pl.program_id(0) % 2 == core_ref[0]
-
-    @pl.when(is_mine)
+    return assemble(mine, *theirs, step_of, core)
+
+
+def assemble_kernel(mine_at, early_at, late_at, is_late, core_ref, mine_ref, early_ref, late_ref, out_ref):
+    part = mine_ref.shape[2]
+    late = is_late[pl.program_id(0)]
+    theirs = jnp.where(late == 1, late_ref[0], early_ref[0])
+
+    @pl.when(core_ref[0] == 0)
     def _():
-        out_ref[...] = mine_ref[0]
-
-    @pl.when(jnp.logical_not(is_mine))
+        out_ref[:, :part] = mine_ref[0]
+        out_ref[:, part:] = theirs
+
+    @pl.when(core_ref[0] == 1)
     def _():
-        out_ref[...] = theirs_ref[0]
-
-
-def assemble(mine, theirs, step_of, core):
+        out_ref[:, :part] = theirs
+        out_ref[:, part:] = mine_ref[0]
+
+
+def assemble(mine, early, late, step_of, core):
     chips, block, part = mine.shape
     devices = 2 * chips
     if part % 128:
         owner = jnp.arange(devices, dtype=jnp.int32)
-        pieces = jnp.concatenate([mine, theirs], axis=0)
+        pieces = jnp.concatenate([mine, early, late], axis=0)
         pieces = pieces[step_of + jnp.where(owner % 2 == core, 0, chips)]
         return jnp.transpose(pieces, (1, 0, 2)).reshape(block, devices * part)
+    half = early.shape[0]
     pairs = step_of.reshape(chips, 2)
-    mine_at = jnp.repeat(jnp.where(core == 0, pairs[:, 0], pairs[:, 1]), 2)
-    theirs_at = jnp.repeat(jnp.where(core == 0, pairs[:, 1], pairs[:, 0]), 2)
+    mine_at = jnp.where(core == 0, pairs[:, 0], pairs[:, 1])
+    theirs_at = jnp.where(core == 0, pairs[:, 1], pairs[:, 0])
+    early_at, late_at = jnp.minimum(theirs_at, half - 1), jnp.maximum(theirs_at - half, 0)
+    is_late = (theirs_at >= half).astype(jnp.int32)
     return pl.pallas_call(
         assemble_kernel,
         grid_spec=pltpu.PrefetchScalarGridSpec(
-            num_scalar_prefetch=3,
-            grid=(devices,),
-            in_specs=[pl.BlockSpec((1, block, part), lambda d, m, t, c: (m[d], 0, 0)),
-                      pl.BlockSpec((1, block, part), lambda d, m, t, c: (t[d], 0, 0))],
-            out_specs=pl.BlockSpec((block, part), lambda d, m, t, c: (0, d)),
+            num_scalar_prefetch=5,
+            grid=(chips,),
+            in_specs=[pl.BlockSpec((1, block, part), lambda d, m, e, l, i, c: (m[d], 0, 0)),
+                      pl.BlockSpec((1, block, part), lambda d, m, e, l, i, c: (e[d], 0, 0)),
+                      pl.BlockSpec((1, block, part), lambda d, m, e, l, i, c: (l[d], 0, 0))],
+            out_specs=pl.BlockSpec((block, 2 * part), lambda d, m, e, l, i, c: (0, d)),
         ),
         out_shape=jax.ShapeDtypeStruct((block, devices * part), jnp.bfloat16),
         cost_estimate=pl.CostEstimate(flops=0, bytes_accessed=4 * block * devices * part, transcendentals=0),
-    )(mine_at, theirs_at, core[None].astype(jnp.int32), mine, theirs)
+    )(mine_at, early_at, late_at, is_late, core[None].astype(jnp.int32), mine, early, late)
 
 
 def solution(mesh):

time: 496 us -> 481 us (0.970); the launches traced: 489 us -> 479 us
  waiting for transfers between devices: 268 us -> 306 us
  other arithmetic: 46.9 us -> 11.3 us
  starting transfers between devices: 58.7 us -> 35 us
  local copies, waits for them, and re-layouts: 10.9 us -> 16.9 us
  Pallas kernels: 59.8 us -> 65.2 us
    ppermute x10 -> x9, waiting for transfers between devices: 179 us -> 271 us  [the longest x7 271 us: shards(): weights.append(lax.ppermute(weights[-1], 'dp', turn))]
    ppermute x6 -> x4, waiting for transfers between devices: 59.2 us -> 17.2 us  [shards(): halos.append((lax.ppermute(pair, 'dp', up), lax.ppermute(pair, 'dp', down)))]
    concatenate x2 -> x0, other arithmetic: 36.4 us -> none  [the longest x1 33 us: shards(): jnp.concatenate([jnp.concatenate(own, axis=1), jnp.concatenate(other, axi...]
    ppermute x10 -> x9, starting transfers between devices: 22.8 us -> 4.64 us  [the longest x7 4.57 us: shards(): weights.append(lax.ppermute(weights[-1], 'dp', turn))]
    ppermute x8, waiting for transfers between devices: 30.5 us -> 17.7 us  [shards(): lax.ppermute(away, 'mp', [(i, (i + k) % groups) for i in range(groups)])]
    pallas_call x3 -> x2, Pallas kernels: 48 us -> 57.1 us  [attend(): pl.pallas_call(functools.partial(attend_kernel, heads=heads, rows=rows),...]
    dynamic_update_slice x0 -> x4, local copies, waits for them, and re-layouts: none -> 7.37 us  [the longest x2 4.16 us: shards(): both = lax.dynamic_update_slice(both, other[None], (1, 0, c * width))]
    ppermute x6 -> x4, starting transfers between devices: 18.3 us -> 13.6 us  [shards(): halos.append((lax.ppermute(pair, 'dp', up), lax.ppermute(pair, 'dp', down)))]
  transfers between devices with their start and end apart: 26 -> 23, of which waited for: 12 -> 9; matrix products, arithmetic and copies ran while one was open for 18% -> 13% of each run, Pallas kernels for 10% -> 12%
where the time goes in v3:
time: 481 us; the launch traced here: 479 us
  waiting for transfers between devices  306 us (64%)
  Pallas kernels  65.2 us (14%)
  matrix products  43.9 us (9%)
  starting transfers between devices  35 us (7%)
  local copies, waits for them, and re-layouts  16.9 us (4%)
  other arithmetic  11.3 us (2%)
    ppermute x7, waiting for transfers between devices, shards(): weights.append(lax.ppermute(weights[-1], 'dp', turn))  271 us
    pallas_call x2, Pallas kernels, attend(): pl.pallas_call(functools.partial(attend_kernel, heads=heads, rows=rows),...  57.1 us
    dot_general x8, matrix products, shards(): jnp.dot(both, weights[step], preferred_element_type=jnp.float32)  43.9 us
    ppermute x8, waiting for transfers between devices, shards(): lax.ppermute(away, 'mp', [(i, (i + k) % groups) for i in range(groups)])  17.7 us
    ppermute x4, waiting for transfers between devices, shards(): halos.append((lax.ppermute(pair, 'dp', up), lax.ppermute(pair, 'dp', down)))  17.2 us
    ppermute x4, starting transfers between devices, shards(): halos.append((lax.ppermute(pair, 'dp', up), lax.ppermute(pair, 'dp', down)))  13.6 us
  transfers between devices with their start and end apart: 23, of which 9 were waited for; matrix products, arithmetic and copies ran while one was open for 13% of the time, Pallas kernels for 12%

profile of v3, /device:TPU:1, one launch (start us, length us, event | category | flops | bytes accessed | tf_op | source)
XLA Modules:
  0.0 478.8 jit_solution(11537858603973583456)
XLA Ops:
  0.0 4.1 fusion.16
  4.1 2.8 pad_maximum_fusion
  6.9 4.5 collective-permute-start
  14.7 2.8 pad_maximum_fusion.1
  17.5 2.4 collective-permute-start.3
  19.9 4.7 collective-permute-start.4
  25.6 163.4 %collective-permute-done.7 = bf16[3072,384]{1,0:T(8,128)(2,1)} collective-permute-done((bf16[3072,384]{1,0:T(8,128)(2,1)S(1)}, bf16[3072,384]{1,0:T(8,128)(2,1)}, u32[]{:S(2)}, u32[]{:S(2)}) %collective-permute-start.7) | collective-permute-done | bytes 2359328 | tf_op jit(solution)/shard_map/ppermute | solution.py:131
  189.1 2.0 collective-permute-start.9
  191.3 2.3 copy-done
  193.6 28.9 %shard_map.64 = bf16[768,1536]{1,0:T(8,128)(2,1)} custom-call(s32[2,3]{1,0:T(2,128)S(1)} %pad_add_fusion.span_ref, bf16[768,3072]{1,0:T(8,128)(2,1)S(1)} %copy-done, bf16[768,3072]{1,0:T(8,128)(2,1)} %collective-permute-done.kb_ref.vb_ref, bf16[768,3072]{1,0:T(8,128)(2,1)} %k_ref.3, bf16[768,3072]{1,0:T(8,128)(2,1)} %collective-permute-done.1.ka_ref.va_ref, ...), custom_call_target="tpu_custom_call" | custom-call | flops 28991029248 | bytes 18874368 | tf_op jit(solution)/shard_map/pallas_call | solution.py:71
  222.5 17.2 %collective-permute-done.3.kb_ref.vb_ref = bf16[768,3072]{1,0:T(8,128)(2,1)} collective-permute-done((bf16[768,3072]{1,0:T(8,128)(2,1)}, bf16[768,3072]{1,0:T(8,128)(2,1)}, u32[]{:S(2)}, u32[]{:S(2)}) %collective-permute-start.3) | collective-permute-done | bytes 4718624 | tf_op jit(solution)/shard_map/ppermute | solution.py:101
  239.7 28.2 %shard_map.65 = bf16[768,1536]{1,0:T(8,128)(2,1)S(1)} custom-call(s32[2,3]{1,0:T(2,128)S(1)} %pad_add_fusion.span_ref, bf16[768,3072]{1,0:T(8,128)(2,1)S(1)} %copy-done, bf16[768,3072]{1,0:T(8,128)(2,1)} %collective-permute-done.3.kb_ref.vb_ref, bf16[768,3072]{1,0:T(8,128)(2,1)} %k_ref.3, bf16[768,3072]{1,0:T(8,128)(2,1)} %collective-permute-done.4.ka_ref.va_ref, ...), custom_call_target="tpu_custom_call" | custom-call | flops 28991029248 | bytes 18874368 | tf_op jit(solution)/shard_map/pallas_call | solution.py:71
  268.0 2.9 dynamic_update_slice.12
  273.5 2.2 bitcast_dynamic-update-slice_fusion
  275.9 5.1 %convolution_convert_fusion.7 = bf16[1536,384]{1,0:T(8,128)(2,1)S(1)} fusion(bf16[1536,3072]{1,0:T(8,128)(2,1)S(1)} %bitcast.113, bf16[3072,384]{1,0:T(8,128)(2,1)S(1)} %copy-done.5), kind=kOutput, calls=%fused_computation.10 | convolution fusion | flops 3624468480 | bytes 12976128 | tf_op jit(solution)/shard_map/dot_general | solution.py:142
  282.3 17.0 %collective-permute-done.11 = bf16[3072,384]{1,0:T(8,128)(2,1)S(1)} collective-permute-done((bf16[3072,384]{1,0:T(8,128)(2,1)}, bf16[3072,384]{1,0:T(8,128)(2,1)S(1)}, u32[]{:S(2)}, u32[]{:S(2)}) %collective-permute-start.11) | collective-permute-done | bytes 2359328 | tf_op jit(solution)/shard_map/ppermute | solution.py:131
  299.5 6.7 %convolution_convert_fusion.6 = bf16[1536,384]{1,0:T(8,128)(2,1)S(1)} fusion(bf16[1536,3072]{1,0:T(8,128)(2,1)S(1)} %bitcast.114, bf16[3072,384]{1,0:T(8,128)(2,1)} %collective-permute-done.7), kind=kOutput, calls=%fused_computation.9 | convolution fusion | flops 3624468480 | bytes 12976128 | tf_op jit(solution)/shard_map/dot_general | solution.py:142
  307.6 6.7 %convolution_convert_fusion.5 = bf16[1536,384]{1,0:T(8,128)(2,1)S(1)} fusion(bf16[1536,3072]{1,0:T(8,128)(2,1)S(1)} %bitcast.115, bf16[3072,384]{1,0:T(8,128)(2,1)} %collective-permute-done.9), kind=kOutput, calls=%fused_computation.8 | convolution fusion | flops 3624468480 | bytes 12976128 | tf_op jit(solution)/shard_map/dot_general | solution.py:142
  314.7 12.7 %collective-permute-done.13 = bf16[3072,384]{1,0:T(8,128)(2,1)S(1)} collective-permute-done((bf16[3072,384]{1,0:T(8,128)(2,1)S(1)}, bf16[3072,384]{1,0:T(8,128)(2,1)S(1)}, u32[]{:S(2)}, u32[]{:S(2)}) %collective-permute-start.13) | collective-permute-done | bytes 2359328 | tf_op jit(solution)/shard_map/ppermute | solution.py:131
  327.7 5.1 %convolution_convert_fusion.4 = bf16[1536,384]{1,0:T(8,128)(2,1)S(1)} fusion(bf16[1536,3072]{1,0:T(8,128)(2,1)S(1)} %bitcast.116, bf16[3072,384]{1,0:T(8,128)(2,1)S(1)} %collective-permute-done.11), kind=kOutput, calls=%fused_computation.7 | convolution fusion | flops 3624468480 | bytes 12976128 | tf_op jit(solution)/shard_map/dot_general | solution.py:142
  334.9 7.1 %collective-permute-done.12 = bf16[2,384,384]{2,1,0:T(8,128)(2,1)S(1)} collective-permute-done((bf16[2,384,384]{2,1,0:T(8,128)(2,1)S(1)}, bf16[2,384,384]{2,1,0:T(8,128)(2,1)S(1)}, u32[]{:S(2)}, u32[]{:S(2)}) %collective-permute-start.12) | collective-permute-done | bytes 589856 | tf_op jit(solution)/shard_map/ppermute | solution.py:147
  342.2 44.7 %collective-permute-done.15 = bf16[3072,384]{1,0:T(8,128)(2,1)S(1)} collective-permute-done((bf16[3072,384]{1,0:T(8,128)(2,1)S(1)}, bf16[3072,384]{1,0:T(8,128)(2,1)S(1)}, u32[]{:S(2)}, u32[]{:S(2)}) %collective-permute-start.15) | collective-permute-done | bytes 2359328 | tf_op jit(solution)/shard_map/ppermute | solution.py:131
  387.4 5.1 %convolution_convert_fusion.3 = bf16[1536,384]{1,0:T(8,128)(2,1)S(1)} fusion(bf16[1536,3072]{1,0:T(8,128)(2,1)S(1)} %bitcast.117, bf16[3072,384]{1,0:T(8,128)(2,1)S(1)} %collective-permute-done.13), kind=kOutput, calls=%fused_computation.6 | convolution fusion | flops 3624468480 | bytes 12976128 | tf_op jit(solution)/shard_map/dot_general | solution.py:142
  393.8 5.1 %convolution_convert_fusion.2 = bf16[1536,384]{1,0:T(8,128)(2,1)S(1)} fusion(bf16[1536,3072]{1,0:T(8,128)(2,1)S(1)} %bitcast.118, bf16[3072,384]{1,0:T(8,128)(2,1)S(1)} %collective-permute-done.15), kind=kOutput, calls=%fused_computation.5 | convolution fusion | flops 3624468480 | bytes 12976128 | tf_op jit(solution)/shard_map/dot_general | solution.py:142
  399.5 4.9 %collective-permute-start.21 = (bf16[4,384,384]{2,1,0:T(8,128)(2,1)S(1)}, bf16[4,384,384]{2,1,0:T(8,128)(2,1)}, u32[]{:S(2)}, u32[]{:S(2)}) collective-permute-start(bf16[4,384,384]{2,1,0:T(8,128)(2,1)S(1)} %pad_maximum_fusion.2), channel_id=1, source_target_pairs={{0,2},{2,0},{4,6},{6,4},{8,10},{10,8},{12,14},{14,12},{16,18},{18,... | collective-permute-start | bytes 3538952 | tf_op jit(solution)/shard_map/ppermute | solution.py:153
  404.4 11.9 %collective-permute-done.17 = bf16[3072,384]{1,0:T(8,128)(2,1)S(1)} collective-permute-done((bf16[3072,384]{1,0:T(8,128)(2,1)S(1)}, bf16[3072,384]{1,0:T(8,128)(2,1)S(1)}, u32[]{:S(2)}, u32[]{:S(2)}) %collective-permute-start.17) | collective-permute-done | bytes 2359328 | tf_op jit(solution)/shard_map/ppermute | solution.py:131
  416.8 5.1 %convolution_convert_fusion.1 = bf16[1536,384]{1,0:T(8,128)(2,1)S(1)} fusion(bf16[1536,3072]{1,0:T(8,128)(2,1)S(1)} %bitcast.119, bf16[3072,384]{1,0:T(8,128)(2,1)S(1)} %collective-permute-done.17), kind=kOutput, calls=%fused_computation.4 | convolution fusion | flops 3624468480 | bytes 12976128 | tf_op jit(solution)/shard_map/dot_general | solution.py:142
  423.3 21.1 %collective-permute-done.19 = bf16[3072,384]{1,0:T(8,128)(2,1)S(1)} collective-permute-done((bf16[3072,384]{1,0:T(8,128)(2,1)S(1)}, bf16[3072,384]{1,0:T(8,128)(2,1)S(1)}, u32[]{:S(2)}, u32[]{:S(2)}) %collective-permute-start.19) | collective-permute-done | bytes 2359328 | tf_op jit(solution)/shard_map/ppermute | solution.py:131
  444.4 5.1 %convolution_convert_fusion = bf16[1536,384]{1,0:T(8,128)(2,1)S(1)} fusion(bf16[1536,3072]{1,0:T(8,128)(2,1)S(1)} %bitcast.120, bf16[3072,384]{1,0:T(8,128)(2,1)S(1)} %collective-permute-done.19), kind=kOutput, calls=%fused_computation.3 | convolution fusion | flops 3624468480 | bytes 12976128 | tf_op jit(solution)/shard_map/dot_general | solution.py:142
  451.2 10.6 %collective-permute-done.20 = bf16[2,384,384]{2,1,0:T(8,128)(2,1)S(1)} collective-permute-done((bf16[2,384,384]{2,1,0:T(8,128)(2,1)S(1)}, bf16[2,384,384]{2,1,0:T(8,128)(2,1)S(1)}, u32[]{:S(2)}, u32[]{:S(2)}) %collective-permute-start.20) | collective-permute-done | bytes 589856 | tf_op jit(solution)/shard_map/ppermute | solution.py:147
  463.4 3.6 collective-permute-start.22
  470.5 8.1 %shard_map.66 = bf16[384,6144]{1,0:T(8,128)(2,1)} custom-call(s32[8]{0:T(128)} %get-tuple-element.29.mine_at, s32[8]{0:T(128)} %get-tuple-element.7.early_at, s32[8]{0:T(128)} %get-tuple-element.6.late_at, s32[8]{0:T(128)} %get-tuple-element.5.is_late, s32[1]{0:T(128)} %bitcast.2.core_ref, bf16[8,384,384]{2,1,0:T(8,128)(2,1)} %copy-done.2, ...), custom_call_target="tpu_custom_call" | custom-call | bytes 9437184 | tf_op jit(solution)/shard_map/pallas_call | solution.py:197
  (97 shorter events, 24.0 us)
Async XLA Ops:
  4.1 9.2 %copy-start.4 = (bf16[3072,384]{1,0:T(8,128)(2,1)S(1)}, bf16[3072,384]{1,0:T(8,128)(2,1)}, u32[]{:S(2)}) copy-start(bf16[3072,384]{1,0:T(8,128)(2,1)} %param.10) | copy-start | bytes 7077892
  6.9 184.2 %collective-permute-start = (bf16[768,3072]{1,0:T(8,128)(2,1)}, bf16[768,3072]{1,0:T(8,128)(2,1)}, u32[]{:S(2)}, u32[]{:S(2)}) collective-permute-start(bf16[768,3072]{1,0:T(8,128)(2,1)} %pad_maximum_fusion), channel_id=1, source_target_pairs={{0,2},{2,4},{4,6},{6,8},{8,10},{10,12},{12,14},{14,16},{16,18},{18... | collective-permute-start | bytes 14155784 | tf_op jit(solution)/shard_map/ppermute | solution.py:101
  11.4 179.7 %collective-permute-start.1 = (bf16[768,3072]{1,0:T(8,128)(2,1)}, bf16[768,3072]{1,0:T(8,128)(2,1)}, u32[]{:S(2)}, u32[]{:S(2)}) collective-permute-start(bf16[768,3072]{1,0:T(8,128)(2,1)} %pad_maximum_fusion), channel_id=1, source_target_pairs={{2,0},{4,2},{6,4},{8,6},{10,8},{12,10},{14,12},{16,14},{18,16},{20... | collective-permute-start | bytes 14155784 | tf_op jit(solution)/shard_map/ppermute | solution.py:101
  13.4 175.7 %collective-permute-start.7 = (bf16[3072,384]{1,0:T(8,128)(2,1)S(1)}, bf16[3072,384]{1,0:T(8,128)(2,1)}, u32[]{:S(2)}, u32[]{:S(2)}) collective-permute-start(bf16[3072,384]{1,0:T(8,128)(2,1)S(1)} %copy-done.4), channel_id=1, source_target_pairs={{0,8},{8,16},{16,24},{24,28},{28,20},{20,12},{12,4},{4,0},{10,2},{... | collective-permute-start | bytes 7077896 | tf_op jit(solution)/shard_map/ppermute | solution.py:131
  14.7 10.0 %copy-start.3 = (s32[64]{0:T(128)S(1)}, s32[64]{0:T(128)}, u32[]{:S(2)}) copy-start(s32[64]{0:T(128)} %param.9) | copy-start | bytes 772
  17.5 222.3 %collective-permute-start.3 = (bf16[768,3072]{1,0:T(8,128)(2,1)}, bf16[768,3072]{1,0:T(8,128)(2,1)}, u32[]{:S(2)}, u32[]{:S(2)}) collective-permute-start(bf16[768,3072]{1,0:T(8,128)(2,1)} %pad_maximum_fusion.1), channel_id=1, source_target_pairs={{0,2},{2,4},{4,6},{6,8},{8,10},{10,12},{12,14},{14,16},{16,18},{18... | collective-permute-start | bytes 14155784 | tf_op jit(solution)/shard_map/ppermute | solution.py:101
  19.9 219.8 %collective-permute-start.4 = (bf16[768,3072]{1,0:T(8,128)(2,1)}, bf16[768,3072]{1,0:T(8,128)(2,1)}, u32[]{:S(2)}, u32[]{:S(2)}) collective-permute-start(bf16[768,3072]{1,0:T(8,128)(2,1)} %pad_maximum_fusion.1), channel_id=1, source_target_pairs={{2,0},{4,2},{6,4},{8,6},{10,8},{12,10},{14,12},{16,14},{18,16},{20... | collective-permute-start | bytes 14155784 | tf_op jit(solution)/shard_map/ppermute | solution.py:101
  189.1 81.8 %collective-permute-start.9 = (bf16[3072,384]{1,0:T(8,128)(2,1)}, bf16[3072,384]{1,0:T(8,128)(2,1)}, u32[]{:S(2)}, u32[]{:S(2)}) collective-permute-start(bf16[3072,384]{1,0:T(8,128)(2,1)} %collective-permute-done.7), channel_id=1, source_target_pairs={{0,8},{8,16},{16,24},{24,28},{28,20},{20,12},{12,4},{4,0},{10,2},{... | collective-permute-start | bytes 7077896 | tf_op jit(solution)/shard_map/ppermute | solution.py:131
  191.3 2.3 copy-start
  222.5 48.6 %collective-permute-start.2 = (bf16[768,1536]{1,0:T(8,128)(2,1)}, bf16[768,1536]{1,0:T(8,128)(2,1)}, u32[]{:S(2)}, u32[]{:S(2)}) collective-permute-start(bf16[768,1536]{1,0:T(8,128)(2,1)} %shard_map.64), channel_id=1, source_target_pairs={{0,2},{2,0},{4,6},{6,4},{8,10},{10,8},{12,14},{14,12},{16,18},{18,... | collective-permute-start | bytes 7077896 | tf_op jit(solution)/shard_map/ppermute | solution.py:135
  267.9 5.6 %collective-permute-start.5 = (bf16[768,1536]{1,0:T(8,128)(2,1)S(1)}, bf16[768,1536]{1,0:T(8,128)(2,1)}, u32[]{:S(2)}, u32[]{:S(2)}) collective-permute-start(bf16[768,1536]{1,0:T(8,128)(2,1)S(1)} %shard_map.65), channel_id=1, source_target_pairs={{0,2},{2,0},{4,6},{6,4},{8,10},{10,8},{12,14},{14,12},{16,18},{18,... | collective-permute-start | bytes 7077896 | tf_op jit(solution)/shard_map/ppermute | solution.py:135
  270.9 28.4 %collective-permute-start.11 = (bf16[3072,384]{1,0:T(8,128)(2,1)}, bf16[3072,384]{1,0:T(8,128)(2,1)S(1)}, u32[]{:S(2)}, u32[]{:S(2)}) collective-permute-start(bf16[3072,384]{1,0:T(8,128)(2,1)} %collective-permute-done.9), channel_id=1, source_target_pairs={{0,8},{8,16},{16,24},{24,28},{28,20},{20,12},{12,4},{4,0},{10,2},{... | collective-permute-start | bytes 7077896 | tf_op jit(solution)/shard_map/ppermute | solution.py:131
  273.5 2.4 copy-start.5
  281.0 53.1 %collective-permute-start.6 = (bf16[2,384,384]{2,1,0:T(8,128)(2,1)S(1)}, bf16[2,384,384]{2,1,0:T(8,128)(2,1)S(1)}, u32[]{:S(2)}, u32[]{:S(2)}) collective-permute-start(bf16[2,384,384]{2,1,0:T(8,128)(2,1)S(1)} %dynamic-slice_bitcast_fusion.7), channel_id=1, source_target_pairs={{0,1},{1,0},{2,3},{3,2},{4,5},{5,4},{6,7},{7,6},{8,9},{9,8},{10,11... | collective-permute-start | bytes 1769480 | tf_op jit(solution)/shard_map/ppermute | solution.py:147
  299.3 28.2 %collective-permute-start.13 = (bf16[3072,384]{1,0:T(8,128)(2,1)S(1)}, bf16[3072,384]{1,0:T(8,128)(2,1)S(1)}, u32[]{:S(2)}, u32[]{:S(2)}) collective-permute-start(bf16[3072,384]{1,0:T(8,128)(2,1)S(1)} %collective-permute-done.11), channel_id=1, source_target_pairs={{0,8},{8,16},{16,24},{24,28},{28,20},{20,12},{12,4},{4,0},{10,2},{... | collective-permute-start | bytes 7077896 | tf_op jit(solution)/shard_map/ppermute | solution.py:131
  306.3 28.1 %collective-permute-start.8 = (bf16[2,384,384]{2,1,0:T(8,128)(2,1)S(1)}, bf16[2,384,384]{2,1,0:T(8,128)(2,1)S(1)}, u32[]{:S(2)}, u32[]{:S(2)}) collective-permute-start(bf16[2,384,384]{2,1,0:T(8,128)(2,1)S(1)} %dynamic-slice_bitcast_fusion.6), channel_id=1, source_target_pairs={{0,1},{1,0},{2,3},{3,2},{4,5},{5,4},{6,7},{7,6},{8,9},{9,8},{10,11... | collective-permute-start | bytes 1769480 | tf_op jit(solution)/shard_map/ppermute | solution.py:147
  314.4 20.2 %collective-permute-start.10 = (bf16[2,384,384]{2,1,0:T(8,128)(2,1)S(1)}, bf16[2,384,384]{2,1,0:T(8,128)(2,1)S(1)}, u32[]{:S(2)}, u32[]{:S(2)}) collective-permute-start(bf16[2,384,384]{2,1,0:T(8,128)(2,1)S(1)} %dynamic-slice_bitcast_fusion.5), channel_id=1, source_target_pairs={{0,1},{1,0},{2,3},{3,2},{4,5},{5,4},{6,7},{7,6},{8,9},{9,8},{10,11... | collective-permute-start | bytes 1769480 | tf_op jit(solution)/shard_map/ppermute | solution.py:147
  327.5 59.4 %collective-permute-start.15 = (bf16[3072,384]{1,0:T(8,128)(2,1)S(1)}, bf16[3072,384]{1,0:T(8,128)(2,1)S(1)}, u32[]{:S(2)}, u32[]{:S(2)}) collective-permute-start(bf16[3072,384]{1,0:T(8,128)(2,1)S(1)} %collective-permute-done.13), channel_id=1, source_target_pairs={{0,8},{8,16},{16,24},{24,28},{28,20},{20,12},{12,4},{4,0},{10,2},{... | collective-permute-start | bytes 7077896 | tf_op jit(solution)/shard_map/ppermute | solution.py:131
  332.9 9.1 %collective-permute-start.12 = (bf16[2,384,384]{2,1,0:T(8,128)(2,1)S(1)}, bf16[2,384,384]{2,1,0:T(8,128)(2,1)S(1)}, u32[]{:S(2)}, u32[]{:S(2)}) collective-permute-start(bf16[2,384,384]{2,1,0:T(8,128)(2,1)S(1)} %dynamic-slice_bitcast_fusion.4), channel_id=1, source_target_pairs={{0,1},{1,0},{2,3},{3,2},{4,5},{5,4},{6,7},{7,6},{8,9},{9,8},{10,11... | collective-permute-start | bytes 1769480 | tf_op jit(solution)/shard_map/ppermute | solution.py:147
  386.9 29.3 %collective-permute-start.17 = (bf16[3072,384]{1,0:T(8,128)(2,1)S(1)}, bf16[3072,384]{1,0:T(8,128)(2,1)S(1)}, u32[]{:S(2)}, u32[]{:S(2)}) collective-permute-start(bf16[3072,384]{1,0:T(8,128)(2,1)S(1)} %collective-permute-done.15), channel_id=1, source_target_pairs={{0,8},{8,16},{16,24},{24,28},{28,20},{20,12},{12,4},{4,0},{10,2},{... | collective-permute-start | bytes 7077896 | tf_op jit(solution)/shard_map/ppermute | solution.py:131
  392.5 23.9 %collective-permute-start.14 = (bf16[2,384,384]{2,1,0:T(8,128)(2,1)S(1)}, bf16[2,384,384]{2,1,0:T(8,128)(2,1)S(1)}, u32[]{:S(2)}, u32[]{:S(2)}) collective-permute-start(bf16[2,384,384]{2,1,0:T(8,128)(2,1)S(1)} %dynamic-slice_bitcast_fusion.3), channel_id=1, source_target_pairs={{0,1},{1,0},{2,3},{3,2},{4,5},{5,4},{6,7},{7,6},{8,9},{9,8},{10,11... | collective-permute-start | bytes 1769480 | tf_op jit(solution)/shard_map/ppermute | solution.py:147
  399.0 17.7 %collective-permute-start.16 = (bf16[2,384,384]{2,1,0:T(8,128)(2,1)S(1)}, bf16[2,384,384]{2,1,0:T(8,128)(2,1)S(1)}, u32[]{:S(2)}, u32[]{:S(2)}) collective-permute-start(bf16[2,384,384]{2,1,0:T(8,128)(2,1)S(1)} %dynamic-slice_bitcast_fusion.2), channel_id=1, source_target_pairs={{0,1},{1,0},{2,3},{3,2},{4,5},{5,4},{6,7},{7,6},{8,9},{9,8},{10,11... | collective-permute-start | bytes 1769480 | tf_op jit(solution)/shard_map/ppermute | solution.py:147
  399.5 71.1 %collective-permute-start.21 = (bf16[4,384,384]{2,1,0:T(8,128)(2,1)S(1)}, bf16[4,384,384]{2,1,0:T(8,128)(2,1)}, u32[]{:S(2)}, u32[]{:S(2)}) collective-permute-start(bf16[4,384,384]{2,1,0:T(8,128)(2,1)S(1)} %pad_maximum_fusion.2), channel_id=1, source_target_pairs={{0,2},{2,0},{4,6},{6,4},{8,10},{10,8},{12,14},{14,12},{16,18},{18,... | collective-permute-start | bytes 3538952 | tf_op jit(solution)/shard_map/ppermute | solution.py:153
  416.2 28.1 %collective-permute-start.19 = (bf16[3072,384]{1,0:T(8,128)(2,1)S(1)}, bf16[3072,384]{1,0:T(8,128)(2,1)S(1)}, u32[]{:S(2)}, u32[]{:S(2)}) collective-permute-start(bf16[3072,384]{1,0:T(8,128)(2,1)S(1)} %collective-permute-done.17), channel_id=1, source_target_pairs={{0,8},{8,16},{16,24},{24,28},{28,20},{20,12},{12,4},{4,0},{10,2},{... | collective-permute-start | bytes 7077896 | tf_op jit(solution)/shard_map/ppermute | solution.py:131
  422.0 28.9 %collective-permute-start.18 = (bf16[2,384,384]{2,1,0:T(8,128)(2,1)S(1)}, bf16[2,384,384]{2,1,0:T(8,128)(2,1)S(1)}, u32[]{:S(2)}, u32[]{:S(2)}) collective-permute-start(bf16[2,384,384]{2,1,0:T(8,128)(2,1)S(1)} %dynamic-slice_bitcast_fusion.1), channel_id=1, source_target_pairs={{0,1},{1,0},{2,3},{3,2},{4,5},{5,4},{6,7},{7,6},{8,9},{9,8},{10,11... | collective-permute-start | bytes 1769480 | tf_op jit(solution)/shard_map/ppermute | solution.py:147
  449.5 12.3 %collective-permute-start.20 = (bf16[2,384,384]{2,1,0:T(8,128)(2,1)S(1)}, bf16[2,384,384]{2,1,0:T(8,128)(2,1)S(1)}, u32[]{:S(2)}, u32[]{:S(2)}) collective-permute-start(bf16[2,384,384]{2,1,0:T(8,128)(2,1)S(1)} %dynamic-slice_bitcast_fusion), channel_id=1, source_target_pairs={{0,1},{1,0},{2,3},{3,2},{4,5},{5,4},{6,7},{7,6},{8,9},{9,8},{10,11... | collective-permute-start | bytes 1769480 | tf_op jit(solution)/shard_map/ppermute | solution.py:147
  451.1 15.8 %copy-start.1 = (s32[8]{0:T(128)S(1)}, s32[8]{0:T(128)}, u32[]{:S(2)}) copy-start(s32[8]{0:T(128)} %constant.191.clone) | copy-start | bytes 100
  462.0 8.5 %copy-start.2 = (bf16[8,384,384]{2,1,0:T(8,128)(2,1)}, bf16[8,384,384]{2,1,0:T(8,128)(2,1)S(1)}, u32[]{:S(2)}) copy-start(bf16[8,384,384]{2,1,0:T(8,128)(2,1)S(1)} %get-tuple-element.19.mine_ref) | copy-start | bytes 7077892
  463.4 7.1 %collective-permute-start.22 = (bf16[4,384,384]{2,1,0:T(8,128)(2,1)}, bf16[4,384,384]{2,1,0:T(8,128)(2,1)}, u32[]{:S(2)}, u32[]{:S(2)}) collective-permute-start(bf16[4,384,384]{2,1,0:T(8,128)(2,1)} %pad_maximum_fusion.3), channel_id=1, source_target_pairs={{0,2},{2,0},{4,6},{6,4},{8,10},{10,8},{12,14},{14,12},{16,18},{18,... | collective-permute-start | bytes 3538952 | tf_op jit(solution)/shard_map/ppermute | solution.py:153

commit v4 on v3

--- a/solution.py
+++ b/solution.py
@@ -131,6 +131,9 @@
         weights.append(lax.ppermute(weights[-1], "dp", turn))
     both = jnp.zeros((2, rows, columns), jnp.bfloat16)
     for c in range(CHUNKS):
+        if c:
+            zero = (weights[min(2 * c, chips - 1)][0, 0].astype(jnp.float32) * 0.0).astype(jnp.int32)
+            span = span + zero
         own = attend(span, queries, keys, values, *halos[c], q_seg, k_seg, c, width)
         other = lax.ppermute(own, "dp", swap)
         both = lax.dynamic_update_slice(both, own[None], (0, 0, c * width))

time: 481 us -> 473 us (0.983); the launches traced: 479 us -> 465 us
  waiting for transfers between devices: 306 us -> 290 us
  starting transfers between devices: 35 us -> 48.3 us
  Pallas kernels: 65.2 us -> 53.5 us
    ppermute x7, waiting for transfers between devices: 271 us -> 247 us  [shards(): weights.append(lax.ppermute(weights[-1], 'dp', turn))]
    ppermute x7, starting transfers between devices: 4.57 us -> 18.9 us  [shards(): weights.append(lax.ppermute(weights[-1], 'dp', turn))]
    pallas_call x2, Pallas kernels: 57.1 us -> 45.4 us  [attend(): pl.pallas_call(functools.partial(attend_kernel, heads=heads, rows=rows),...]
    ppermute x4, waiting for transfers between devices: 17.2 us -> 23.3 us  [shards(): halos.append((lax.ppermute(pair, 'dp', up), lax.ppermute(pair, 'dp', down)))]
  transfers between devices with their start and end apart: 23 -> 23, of which waited for: 9 -> 10; matrix products, arithmetic and copies ran while one was open for 13% -> 15% of each run, Pallas kernels for 12% -> 10%
where the time goes in v4:
time: 473 us; the launch traced here: 465 us
  waiting for transfers between devices  290 us (61%)
  Pallas kernels  53.5 us (11%)
  starting transfers between devices  48.3 us (10%)
  matrix products  42.2 us (9%)
  local copies, waits for them, and re-layouts  18 us (4%)
  other arithmetic  11.1 us (2%)
    ppermute x7, waiting for transfers between devices, shards(): weights.append(lax.ppermute(weights[-1], 'dp', turn))  247 us
    pallas_call x2, Pallas kernels, attend(): pl.pallas_call(functools.partial(attend_kernel, heads=heads, rows=rows),...  45.4 us
    dot_general x8, matrix products, shards(): jnp.dot(both, weights[step], preferred_element_type=jnp.float32)  42.2 us
    ppermute x4, waiting for transfers between devices, shards(): halos.append((lax.ppermute(pair, 'dp', up), lax.ppermute(pair, 'dp', down)))  23.3 us
    ppermute x8, waiting for transfers between devices, shards(): lax.ppermute(away, 'mp', [(i, (i + k) % groups) for i in range(groups)])  19.5 us
    ppermute x7, starting transfers between devices, shards(): weights.append(lax.ppermute(weights[-1], 'dp', turn))  18.9 us
    ppermute x4, starting transfers between devices, shards(): halos.append((lax.ppermute(pair, 'dp', up), lax.ppermute(pair, 'dp', down)))  12.9 us
  transfers between devices with their start and end apart: 23, of which 10 were waited for; matrix products, arithmetic and copies ran while one was open for 15% of the time, Pallas kernels for 10%

profile of v4, /device:TPU:1, one launch (start us, length us, event | category | flops | bytes accessed | tf_op | source)
XLA Modules:
  0.0 464.6 jit_solution(5899618803002468355)
XLA Ops:
  2.1 4.1 fusion.16
  6.2 2.8 pad_maximum_fusion
  8.9 2.5 collective-permute-start
  11.4 4.0 collective-permute-start.1
  15.4 22.6 %collective-permute-done.3 = bf16[3072,384]{1,0:T(8,128)(2,1)S(1)} collective-permute-done((bf16[3072,384]{1,0:T(8,128)(2,1)}, bf16[3072,384]{1,0:T(8,128)(2,1)S(1)}, u32[]{:S(2)}, u32[]{:S(2)}) %collective-permute-start.3) | collective-permute-done | bytes 2359328 | tf_op jit(solution)/shard_map/ppermute | solution.py:131
  38.0 5.0 %collective-permute-start.4 = (bf16[3072,384]{1,0:T(8,128)(2,1)S(1)}, bf16[3072,384]{1,0:T(8,128)(2,1)}, u32[]{:S(2)}, u32[]{:S(2)}) collective-permute-start(bf16[3072,384]{1,0:T(8,128)(2,1)S(1)} %collective-permute-done.3), channel_id=1, source_target_pairs={{0,8},{8,16},{16,24},{24,28},{28,20},{20,12},{12,4},{4,0},{10,2},{... | collective-permute-start | bytes 7077896 | tf_op jit(solution)/shard_map/ppermute | solution.py:131
  43.0 2.8 pad_maximum_fusion.1
  47.8 4.5 collective-permute-start.6
  53.3 151.8 %collective-permute-done.4 = bf16[3072,384]{1,0:T(8,128)(2,1)} collective-permute-done((bf16[3072,384]{1,0:T(8,128)(2,1)S(1)}, bf16[3072,384]{1,0:T(8,128)(2,1)}, u32[]{:S(2)}, u32[]{:S(2)}) %collective-permute-start.4) | collective-permute-done | bytes 2359328 | tf_op jit(solution)/shard_map/ppermute | solution.py:131
  209.4 23.1 %shard_map.64 = bf16[768,1536]{1,0:T(8,128)(2,1)} custom-call(s32[2,3]{1,0:T(2,128)S(1)} %get-tuple-element.31.span_ref, bf16[768,3072]{1,0:T(8,128)(2,1)S(1)} %copy-done, bf16[768,3072]{1,0:T(8,128)(2,1)} %collective-permute-done.kb_ref.vb_ref, bf16[768,3072]{1,0:T(8,128)(2,1)} %k_ref.3, bf16[768,3072]{1,0:T(8,128)(2,1)} %collective-permute-done.1.ka_ref.va_ref, ...), custom_call_target="tpu_custom_call" | custom-call | flops 28991029248 | bytes 18874368 | tf_op jit(solution)/shard_map/pallas_call | solution.py:71
  232.4 23.3 %collective-permute-done.5.kb_ref.vb_ref = bf16[768,3072]{1,0:T(8,128)(2,1)} collective-permute-done((bf16[768,3072]{1,0:T(8,128)(2,1)}, bf16[768,3072]{1,0:T(8,128)(2,1)}, u32[]{:S(2)}, u32[]{:S(2)}) %collective-permute-start.5) | collective-permute-done | bytes 4718624 | tf_op jit(solution)/shard_map/ppermute | solution.py:101
  255.7 22.4 %shard_map.65 = bf16[768,1536]{1,0:T(8,128)(2,1)S(1)} custom-call(s32[2,3]{1,0:T(2,128)S(1)} %get-tuple-element.30.span_ref, bf16[768,3072]{1,0:T(8,128)(2,1)S(1)} %copy-done, bf16[768,3072]{1,0:T(8,128)(2,1)} %collective-permute-done.5.kb_ref.vb_ref, bf16[768,3072]{1,0:T(8,128)(2,1)} %k_ref.3, bf16[768,3072]{1,0:T(8,128)(2,1)} %collective-permute-done.6.ka_ref.va_ref, ...), custom_call_target="tpu_custom_call" | custom-call | flops 28991029248 | bytes 18874368 | tf_op jit(solution)/shard_map/pallas_call | solution.py:71
  278.2 2.9 dynamic_update_slice.12
  281.0 6.6 %collective-permute-start.11 = (bf16[3072,384]{1,0:T(8,128)(2,1)}, bf16[3072,384]{1,0:T(8,128)(2,1)S(1)}, u32[]{:S(2)}, u32[]{:S(2)}) collective-permute-start(bf16[3072,384]{1,0:T(8,128)(2,1)} %collective-permute-done.4), channel_id=1, source_target_pairs={{0,8},{8,16},{16,24},{24,28},{28,20},{20,12},{12,4},{4,0},{10,2},{... | collective-permute-start | bytes 7077896 | tf_op jit(solution)/shard_map/ppermute | solution.py:131
  292.4 5.1 %convolution_convert_fusion.7 = bf16[1536,384]{1,0:T(8,128)(2,1)S(1)} fusion(bf16[1536,3072]{1,0:T(8,128)(2,1)S(1)} %bitcast.114, bf16[3072,384]{1,0:T(8,128)(2,1)S(1)} %copy-done.4), kind=kOutput, calls=%fused_computation.10 | convolution fusion | flops 3624468480 | bytes 12976128 | tf_op jit(solution)/shard_map/dot_general | solution.py:145
  298.8 14.9 %collective-permute-done.11 = bf16[3072,384]{1,0:T(8,128)(2,1)S(1)} collective-permute-done((bf16[3072,384]{1,0:T(8,128)(2,1)}, bf16[3072,384]{1,0:T(8,128)(2,1)S(1)}, u32[]{:S(2)}, u32[]{:S(2)}) %collective-permute-start.11) | collective-permute-done | bytes 2359328 | tf_op jit(solution)/shard_map/ppermute | solution.py:131
  316.0 5.1 %convolution_convert_fusion.6 = bf16[1536,384]{1,0:T(8,128)(2,1)S(1)} fusion(bf16[1536,3072]{1,0:T(8,128)(2,1)S(1)} %bitcast.115, bf16[3072,384]{1,0:T(8,128)(2,1)S(1)} %copy-done.6), kind=kOutput, calls=%fused_computation.9 | convolution fusion | flops 3624468480 | bytes 12976128 | tf_op jit(solution)/shard_map/dot_general | solution.py:145
  322.5 6.7 %convolution_convert_fusion.5 = bf16[1536,384]{1,0:T(8,128)(2,1)S(1)} fusion(bf16[1536,3072]{1,0:T(8,128)(2,1)S(1)} %bitcast.116, bf16[3072,384]{1,0:T(8,128)(2,1)} %collective-permute-done.4), kind=kOutput, calls=%fused_computation.8 | convolution fusion | flops 3624468480 | bytes 12976128 | tf_op jit(solution)/shard_map/dot_general | solution.py:145
  329.6 12.3 %collective-permute-done.13 = bf16[3072,384]{1,0:T(8,128)(2,1)S(1)} collective-permute-done((bf16[3072,384]{1,0:T(8,128)(2,1)S(1)}, bf16[3072,384]{1,0:T(8,128)(2,1)S(1)}, u32[]{:S(2)}, u32[]{:S(2)}) %collective-permute-start.13) | collective-permute-done | bytes 2359328 | tf_op jit(solution)/shard_map/ppermute | solution.py:131
  344.3 5.1 %convolution_convert_fusion.4 = bf16[1536,384]{1,0:T(8,128)(2,1)S(1)} fusion(bf16[1536,3072]{1,0:T(8,128)(2,1)S(1)} %bitcast.117, bf16[3072,384]{1,0:T(8,128)(2,1)S(1)} %collective-permute-done.11), kind=kOutput, calls=%fused_computation.7 | convolution fusion | flops 3624468480 | bytes 12976128 | tf_op jit(solution)/shard_map/dot_general | solution.py:145
  351.4 8.8 %collective-permute-done.12 = bf16[2,384,384]{2,1,0:T(8,128)(2,1)S(1)} collective-permute-done((bf16[2,384,384]{2,1,0:T(8,128)(2,1)S(1)}, bf16[2,384,384]{2,1,0:T(8,128)(2,1)S(1)}, u32[]{:S(2)}, u32[]{:S(2)}) %collective-permute-start.12) | collective-permute-done | bytes 589856 | tf_op jit(solution)/shard_map/ppermute | solution.py:150
  360.5 12.6 %collective-permute-done.15 = bf16[3072,384]{1,0:T(8,128)(2,1)S(1)} collective-permute-done((bf16[3072,384]{1,0:T(8,128)(2,1)S(1)}, bf16[3072,384]{1,0:T(8,128)(2,1)S(1)}, u32[]{:S(2)}, u32[]{:S(2)}) %collective-permute-start.15) | collective-permute-done | bytes 2359328 | tf_op jit(solution)/shard_map/ppermute | solution.py:131
  373.6 5.1 %convolution_convert_fusion.3 = bf16[1536,384]{1,0:T(8,128)(2,1)S(1)} fusion(bf16[1536,3072]{1,0:T(8,128)(2,1)S(1)} %bitcast.118, bf16[3072,384]{1,0:T(8,128)(2,1)S(1)} %collective-permute-done.13), kind=kOutput, calls=%fused_computation.6 | convolution fusion | flops 3624468480 | bytes 12976128 | tf_op jit(solution)/shard_map/dot_general | solution.py:145
  380.0 5.1 %convolution_convert_fusion.2 = bf16[1536,384]{1,0:T(8,128)(2,1)S(1)} fusion(bf16[1536,3072]{1,0:T(8,128)(2,1)S(1)} %bitcast.119, bf16[3072,384]{1,0:T(8,128)(2,1)S(1)} %collective-permute-done.15), kind=kOutput, calls=%fused_computation.5 | convolution fusion | flops 3624468480 | bytes 12976128 | tf_op jit(solution)/shard_map/dot_general | solution.py:145
  385.7 4.6 collective-permute-start.21
  390.3 11.9 %collective-permute-done.17 = bf16[3072,384]{1,0:T(8,128)(2,1)S(1)} collective-permute-done((bf16[3072,384]{1,0:T(8,128)(2,1)S(1)}, bf16[3072,384]{1,0:T(8,128)(2,1)S(1)}, u32[]{:S(2)}, u32[]{:S(2)}) %collective-permute-start.17) | collective-permute-done | bytes 2359328 | tf_op jit(solution)/shard_map/ppermute | solution.py:131
  402.8 5.1 %convolution_convert_fusion.1 = bf16[1536,384]{1,0:T(8,128)(2,1)S(1)} fusion(bf16[1536,3072]{1,0:T(8,128)(2,1)S(1)} %bitcast.120, bf16[3072,384]{1,0:T(8,128)(2,1)S(1)} %collective-permute-done.17), kind=kOutput, calls=%fused_computation.4 | convolution fusion | flops 3624468480 | bytes 12976128 | tf_op jit(solution)/shard_map/dot_general | solution.py:145
  409.2 21.1 %collective-permute-done.19 = bf16[3072,384]{1,0:T(8,128)(2,1)S(1)} collective-permute-done((bf16[3072,384]{1,0:T(8,128)(2,1)S(1)}, bf16[3072,384]{1,0:T(8,128)(2,1)S(1)}, u32[]{:S(2)}, u32[]{:S(2)}) %collective-permute-start.19) | collective-permute-done | bytes 2359328 | tf_op jit(solution)/shard_map/ppermute | solution.py:131
  430.3 5.1 %convolution_convert_fusion = bf16[1536,384]{1,0:T(8,128)(2,1)S(1)} fusion(bf16[1536,3072]{1,0:T(8,128)(2,1)S(1)} %bitcast.121, bf16[3072,384]{1,0:T(8,128)(2,1)S(1)} %collective-permute-done.19), kind=kOutput, calls=%fused_computation.3 | convolution fusion | flops 3624468480 | bytes 12976128 | tf_op jit(solution)/shard_map/dot_general | solution.py:145
  437.1 10.6 %collective-permute-done.20 = bf16[2,384,384]{2,1,0:T(8,128)(2,1)S(1)} collective-permute-done((bf16[2,384,384]{2,1,0:T(8,128)(2,1)S(1)}, bf16[2,384,384]{2,1,0:T(8,128)(2,1)S(1)}, u32[]{:S(2)}, u32[]{:S(2)}) %collective-permute-start.20) | collective-permute-done | bytes 589856 | tf_op jit(solution)/shard_map/ppermute | solution.py:150
  449.3 3.5 collective-permute-start.22
  456.3 8.1 %shard_map.66 = bf16[384,6144]{1,0:T(8,128)(2,1)} custom-call(s32[8]{0:T(128)} %get-tuple-element.29.mine_at, s32[8]{0:T(128)} %get-tuple-element.7.early_at, s32[8]{0:T(128)} %get-tuple-element.6.late_at, s32[8]{0:T(128)} %get-tuple-element.5.is_late, s32[1]{0:T(128)} %bitcast.2.core_ref, bf16[8,384,384]{2,1,0:T(8,128)(2,1)} %copy-done.2, ...), custom_call_target="tpu_custom_call" | custom-call | bytes 9437184 | tf_op jit(solution)/shard_map/pallas_call | solution.py:200
  (100 shorter events, 34.2 us)
Async XLA Ops:
  0.0 38.0 %collective-permute-start.3 = (bf16[3072,384]{1,0:T(8,128)(2,1)}, bf16[3072,384]{1,0:T(8,128)(2,1)S(1)}, u32[]{:S(2)}, u32[]{:S(2)}) collective-permute-start(bf16[3072,384]{1,0:T(8,128)(2,1)} %param.10), channel_id=1, source_target_pairs={{0,8},{8,16},{16,24},{24,28},{28,20},{20,12},{12,4},{4,0},{10,2},{... | collective-permute-start | bytes 7077896 | tf_op jit(solution)/shard_map/ppermute | solution.py:131
  8.9 197.9 %collective-permute-start = (bf16[768,3072]{1,0:T(8,128)(2,1)}, bf16[768,3072]{1,0:T(8,128)(2,1)}, u32[]{:S(2)}, u32[]{:S(2)}) collective-permute-start(bf16[768,3072]{1,0:T(8,128)(2,1)} %pad_maximum_fusion), channel_id=1, source_target_pairs={{0,2},{2,4},{4,6},{6,8},{8,10},{10,12},{12,14},{14,16},{16,18},{18... | collective-permute-start | bytes 14155784 | tf_op jit(solution)/shard_map/ppermute | solution.py:101
  11.4 195.4 %collective-permute-start.1 = (bf16[768,3072]{1,0:T(8,128)(2,1)}, bf16[768,3072]{1,0:T(8,128)(2,1)}, u32[]{:S(2)}, u32[]{:S(2)}) collective-permute-start(bf16[768,3072]{1,0:T(8,128)(2,1)} %pad_maximum_fusion), channel_id=1, source_target_pairs={{2,0},{4,2},{6,4},{8,6},{10,8},{12,10},{14,12},{16,14},{18,16},{20... | collective-permute-start | bytes 14155784 | tf_op jit(solution)/shard_map/ppermute | solution.py:101
  38.0 7.8 %copy-start.5 = (bf16[3072,384]{1,0:T(8,128)(2,1)}, bf16[3072,384]{1,0:T(8,128)(2,1)S(1)}, u32[]{:S(2)}) copy-start(bf16[3072,384]{1,0:T(8,128)(2,1)S(1)} %collective-permute-done.3) | copy-start | bytes 7077892
  38.0 167.0 %collective-permute-start.4 = (bf16[3072,384]{1,0:T(8,128)(2,1)S(1)}, bf16[3072,384]{1,0:T(8,128)(2,1)}, u32[]{:S(2)}, u32[]{:S(2)}) collective-permute-start(bf16[3072,384]{1,0:T(8,128)(2,1)S(1)} %collective-permute-done.3), channel_id=1, source_target_pairs={{0,8},{8,16},{16,24},{24,28},{28,20},{20,12},{12,4},{4,0},{10,2},{... | collective-permute-start | bytes 7077896 | tf_op jit(solution)/shard_map/ppermute | solution.py:131
  43.0 9.3 %copy-start.3 = (s32[64]{0:T(128)S(1)}, s32[64]{0:T(128)}, u32[]{:S(2)}) copy-start(s32[64]{0:T(128)} %param.9) | copy-start | bytes 772
  45.8 209.9 %collective-permute-start.5 = (bf16[768,3072]{1,0:T(8,128)(2,1)}, bf16[768,3072]{1,0:T(8,128)(2,1)}, u32[]{:S(2)}, u32[]{:S(2)}) collective-permute-start(bf16[768,3072]{1,0:T(8,128)(2,1)} %pad_maximum_fusion.1), channel_id=1, source_target_pairs={{0,2},{2,4},{4,6},{6,8},{8,10},{10,12},{12,14},{14,16},{16,18},{18... | collective-permute-start | bytes 14155784 | tf_op jit(solution)/shard_map/ppermute | solution.py:101
  47.8 207.9 %collective-permute-start.6 = (bf16[768,3072]{1,0:T(8,128)(2,1)}, bf16[768,3072]{1,0:T(8,128)(2,1)}, u32[]{:S(2)}, u32[]{:S(2)}) collective-permute-start(bf16[768,3072]{1,0:T(8,128)(2,1)} %pad_maximum_fusion.1), channel_id=1, source_target_pairs={{2,0},{4,2},{6,4},{8,6},{10,8},{12,10},{14,12},{16,14},{18,16},{20... | collective-permute-start | bytes 14155784 | tf_op jit(solution)/shard_map/ppermute | solution.py:101
  207.0 2.3 copy-start
  232.4 55.2 %collective-permute-start.2 = (bf16[768,1536]{1,0:T(8,128)(2,1)}, bf16[768,1536]{1,0:T(8,128)(2,1)}, u32[]{:S(2)}, u32[]{:S(2)}) collective-permute-start(bf16[768,1536]{1,0:T(8,128)(2,1)} %shard_map.64), channel_id=1, source_target_pairs={{0,2},{2,0},{4,6},{6,4},{8,10},{10,8},{12,14},{14,12},{16,18},{18,... | collective-permute-start | bytes 7077896 | tf_op jit(solution)/shard_map/ppermute | solution.py:138
  278.1 12.0 %collective-permute-start.7 = (bf16[768,1536]{1,0:T(8,128)(2,1)S(1)}, bf16[768,1536]{1,0:T(8,128)(2,1)}, u32[]{:S(2)}, u32[]{:S(2)}) collective-permute-start(bf16[768,1536]{1,0:T(8,128)(2,1)S(1)} %shard_map.65), channel_id=1, source_target_pairs={{0,2},{2,0},{4,6},{6,4},{8,10},{10,8},{12,14},{14,12},{16,18},{18,... | collective-permute-start | bytes 7077896 | tf_op jit(solution)/shard_map/ppermute | solution.py:138
  281.0 32.7 %collective-permute-start.11 = (bf16[3072,384]{1,0:T(8,128)(2,1)}, bf16[3072,384]{1,0:T(8,128)(2,1)S(1)}, u32[]{:S(2)}, u32[]{:S(2)}) collective-permute-start(bf16[3072,384]{1,0:T(8,128)(2,1)} %collective-permute-done.4), channel_id=1, source_target_pairs={{0,8},{8,16},{16,24},{24,28},{28,20},{20,12},{12,4},{4,0},{10,2},{... | collective-permute-start | bytes 7077896 | tf_op jit(solution)/shard_map/ppermute | solution.py:131
  290.0 2.4 copy-start.4
  292.4 23.6 %copy-start.6 = (bf16[3072,384]{1,0:T(8,128)(2,1)S(1)}, bf16[3072,384]{1,0:T(8,128)(2,1)}, u32[]{:S(2)}) copy-start(bf16[3072,384]{1,0:T(8,128)(2,1)} %copy-done.5) | copy-start | bytes 7077892
  297.6 53.1 %collective-permute-start.8 = (bf16[2,384,384]{2,1,0:T(8,128)(2,1)S(1)}, bf16[2,384,384]{2,1,0:T(8,128)(2,1)S(1)}, u32[]{:S(2)}, u32[]{:S(2)}) collective-permute-start(bf16[2,384,384]{2,1,0:T(8,128)(2,1)S(1)} %dynamic-slice_bitcast_fusion.7), channel_id=1, source_target_pairs={{0,1},{1,0},{2,3},{3,2},{4,5},{5,4},{6,7},{7,6},{8,9},{9,8},{10,11... | collective-permute-start | bytes 1769480 | tf_op jit(solution)/shard_map/ppermute | solution.py:150
  313.8 28.2 %collective-permute-start.13 = (bf16[3072,384]{1,0:T(8,128)(2,1)S(1)}, bf16[3072,384]{1,0:T(8,128)(2,1)S(1)}, u32[]{:S(2)}, u32[]{:S(2)}) collective-permute-start(bf16[3072,384]{1,0:T(8,128)(2,1)S(1)} %collective-permute-done.11), channel_id=1, source_target_pairs={{0,8},{8,16},{16,24},{24,28},{28,20},{20,12},{12,4},{4,0},{10,2},{... | collective-permute-start | bytes 7077896 | tf_op jit(solution)/shard_map/ppermute | solution.py:131
  321.2 29.7 %collective-permute-start.9 = (bf16[2,384,384]{2,1,0:T(8,128)(2,1)S(1)}, bf16[2,384,384]{2,1,0:T(8,128)(2,1)S(1)}, u32[]{:S(2)}, u32[]{:S(2)}) collective-permute-start(bf16[2,384,384]{2,1,0:T(8,128)(2,1)S(1)} %dynamic-slice_bitcast_fusion.6), channel_id=1, source_target_pairs={{0,1},{1,0},{2,3},{3,2},{4,5},{5,4},{6,7},{7,6},{8,9},{9,8},{10,11... | collective-permute-start | bytes 1769480 | tf_op jit(solution)/shard_map/ppermute | solution.py:150
  329.3 21.9 %collective-permute-start.10 = (bf16[2,384,384]{2,1,0:T(8,128)(2,1)S(1)}, bf16[2,384,384]{2,1,0:T(8,128)(2,1)S(1)}, u32[]{:S(2)}, u32[]{:S(2)}) collective-permute-start(bf16[2,384,384]{2,1,0:T(8,128)(2,1)S(1)} %dynamic-slice_bitcast_fusion.5), channel_id=1, source_target_pairs={{0,1},{1,0},{2,3},{3,2},{4,5},{5,4},{6,7},{7,6},{8,9},{9,8},{10,11... | collective-permute-start | bytes 1769480 | tf_op jit(solution)/shard_map/ppermute | solution.py:150
  341.9 31.2 %collective-permute-start.15 = (bf16[3072,384]{1,0:T(8,128)(2,1)S(1)}, bf16[3072,384]{1,0:T(8,128)(2,1)S(1)}, u32[]{:S(2)}, u32[]{:S(2)}) collective-permute-start(bf16[3072,384]{1,0:T(8,128)(2,1)S(1)} %collective-permute-done.13), channel_id=1, source_target_pairs={{0,8},{8,16},{16,24},{24,28},{28,20},{20,12},{12,4},{4,0},{10,2},{... | collective-permute-start | bytes 7077896 | tf_op jit(solution)/shard_map/ppermute | solution.py:131
  349.4 10.9 %collective-permute-start.12 = (bf16[2,384,384]{2,1,0:T(8,128)(2,1)S(1)}, bf16[2,384,384]{2,1,0:T(8,128)(2,1)S(1)}, u32[]{:S(2)}, u32[]{:S(2)}) collective-permute-start(bf16[2,384,384]{2,1,0:T(8,128)(2,1)S(1)} %dynamic-slice_bitcast_fusion.4), channel_id=1, source_target_pairs={{0,1},{1,0},{2,3},{3,2},{4,5},{5,4},{6,7},{7,6},{8,9},{9,8},{10,11... | collective-permute-start | bytes 1769480 | tf_op jit(solution)/shard_map/ppermute | solution.py:150
  373.1 29.0 %collective-permute-start.17 = (bf16[3072,384]{1,0:T(8,128)(2,1)S(1)}, bf16[3072,384]{1,0:T(8,128)(2,1)S(1)}, u32[]{:S(2)}, u32[]{:S(2)}) collective-permute-start(bf16[3072,384]{1,0:T(8,128)(2,1)S(1)} %collective-permute-done.15), channel_id=1, source_target_pairs={{0,8},{8,16},{16,24},{24,28},{28,20},{20,12},{12,4},{4,0},{10,2},{... | collective-permute-start | bytes 7077896 | tf_op jit(solution)/shard_map/ppermute | solution.py:131
  378.7 23.6 %collective-permute-start.14 = (bf16[2,384,384]{2,1,0:T(8,128)(2,1)S(1)}, bf16[2,384,384]{2,1,0:T(8,128)(2,1)S(1)}, u32[]{:S(2)}, u32[]{:S(2)}) collective-permute-start(bf16[2,384,384]{2,1,0:T(8,128)(2,1)S(1)} %dynamic-slice_bitcast_fusion.3), channel_id=1, source_target_pairs={{0,1},{1,0},{2,3},{3,2},{4,5},{5,4},{6,7},{7,6},{8,9},{9,8},{10,11... | collective-permute-start | bytes 1769480 | tf_op jit(solution)/shard_map/ppermute | solution.py:150
  385.2 17.4 %collective-permute-start.16 = (bf16[2,384,384]{2,1,0:T(8,128)(2,1)S(1)}, bf16[2,384,384]{2,1,0:T(8,128)(2,1)S(1)}, u32[]{:S(2)}, u32[]{:S(2)}) collective-permute-start(bf16[2,384,384]{2,1,0:T(8,128)(2,1)S(1)} %dynamic-slice_bitcast_fusion.2), channel_id=1, source_target_pairs={{0,1},{1,0},{2,3},{3,2},{4,5},{5,4},{6,7},{7,6},{8,9},{9,8},{10,11... | collective-permute-start | bytes 1769480 | tf_op jit(solution)/shard_map/ppermute | solution.py:150
  385.7 70.6 %collective-permute-start.21 = (bf16[4,384,384]{2,1,0:T(8,128)(2,1)S(1)}, bf16[4,384,384]{2,1,0:T(8,128)(2,1)}, u32[]{:S(2)}, u32[]{:S(2)}) collective-permute-start(bf16[4,384,384]{2,1,0:T(8,128)(2,1)S(1)} %pad_maximum_fusion.2), channel_id=1, source_target_pairs={{0,2},{2,0},{4,6},{6,4},{8,10},{10,8},{12,14},{14,12},{16,18},{18,... | collective-permute-start | bytes 3538952 | tf_op jit(solution)/shard_map/ppermute | solution.py:156
  402.2 28.1 %collective-permute-start.19 = (bf16[3072,384]{1,0:T(8,128)(2,1)S(1)}, bf16[3072,384]{1,0:T(8,128)(2,1)S(1)}, u32[]{:S(2)}, u32[]{:S(2)}) collective-permute-start(bf16[3072,384]{1,0:T(8,128)(2,1)S(1)} %collective-permute-done.17), channel_id=1, source_target_pairs={{0,8},{8,16},{16,24},{24,28},{28,20},{20,12},{12,4},{4,0},{10,2},{... | collective-permute-start | bytes 7077896 | tf_op jit(solution)/shard_map/ppermute | solution.py:131
  407.9 28.9 %collective-permute-start.18 = (bf16[2,384,384]{2,1,0:T(8,128)(2,1)S(1)}, bf16[2,384,384]{2,1,0:T(8,128)(2,1)S(1)}, u32[]{:S(2)}, u32[]{:S(2)}) collective-permute-start(bf16[2,384,384]{2,1,0:T(8,128)(2,1)S(1)} %dynamic-slice_bitcast_fusion.1), channel_id=1, source_target_pairs={{0,1},{1,0},{2,3},{3,2},{4,5},{5,4},{6,7},{7,6},{8,9},{9,8},{10,11... | collective-permute-start | bytes 1769480 | tf_op jit(solution)/shard_map/ppermute | solution.py:150
  435.5 12.3 %collective-permute-start.20 = (bf16[2,384,384]{2,1,0:T(8,128)(2,1)S(1)}, bf16[2,384,384]{2,1,0:T(8,128)(2,1)S(1)}, u32[]{:S(2)}, u32[]{:S(2)}) collective-permute-start(bf16[2,384,384]{2,1,0:T(8,128)(2,1)S(1)} %dynamic-slice_bitcast_fusion), channel_id=1, source_target_pairs={{0,1},{1,0},{2,3},{3,2},{4,5},{5,4},{6,7},{7,6},{8,9},{9,8},{10,11... | collective-permute-start | bytes 1769480 | tf_op jit(solution)/shard_map/ppermute | solution.py:150
  437.1 15.8 %copy-start.1 = (s32[8]{0:T(128)S(1)}, s32[8]{0:T(128)}, u32[]{:S(2)}) copy-start(s32[8]{0:T(128)} %constant.194.clone) | copy-start | bytes 100
  447.9 8.3 %copy-start.2 = (bf16[8,384,384]{2,1,0:T(8,128)(2,1)}, bf16[8,384,384]{2,1,0:T(8,128)(2,1)S(1)}, u32[]{:S(2)}) copy-start(bf16[8,384,384]{2,1,0:T(8,128)(2,1)S(1)} %get-tuple-element.19.mine_ref) | copy-start | bytes 7077892
  449.3 7.0 %collective-permute-start.22 = (bf16[4,384,384]{2,1,0:T(8,128)(2,1)}, bf16[4,384,384]{2,1,0:T(8,128)(2,1)}, u32[]{:S(2)}, u32[]{:S(2)}) collective-permute-start(bf16[4,384,384]{2,1,0:T(8,128)(2,1)} %pad_maximum_fusion.3), channel_id=1, source_target_pairs={{0,2},{2,0},{4,6},{6,4},{8,10},{10,8},{12,14},{14,12},{16,18},{18,... | collective-permute-start | bytes 3538952 | tf_op jit(solution)/shard_map/ppermute | solution.py:156
